TPU v7x, 128 devices: a whole 4x4x4 slice. The times are simulated.
128 devices in a mesh: gx: 16 (over x, z), gy: 8 (over y, core).
Axes of the slice: x: 4, y: 4, z: 4, core: 2. Of those that a mesh axis runs over, the one named last changes fastest.
Arguments:
- particle_pos: float32 [3, 2097152], P(None, ('gx', 'gy')), may hold values from 0 to 16
- tile_dest: int32 [16384, 1], P(('gx', 'gy')), may hold values from 0 to 127; in each aligned block of 128 rows (0 to 127, 128 to 255, ...) at most 2 rows name the same one
- tile_block: int32 [16384], P(('gx', 'gy')), may hold values from 0 to 127
- fluid_flag: int32 [512, 512, 256], P('gx', 'gy'), may hold values 0 or 1
- divergence: float32 [512, 512, 256], P('gx', 'gy'), may hold values from -6 to 6
Outputs:
- level_set: float32 [512, 512, 256], P('gx', 'gy')
- pressure: float32 [512, 512, 256], P('gx', 'gy')
Inputs may be any that keep to these rules, and one draw needn't show every extreme that they name: `tile_dest`: among the tiles of one device, no brick is named more than 2 times, a bound that some block reaches.
All inputs are finite; a program needn't handle non-finite values. No bound on the sum of `fluid_flag` on one device may be relied on, other than what follows from the above.
Results may differ from a plain program's by a relative error of at most 0.00002.
Values sent between devices are 32-bit elements; how exact they have to be, the bound alone decides.
No kernel may reach another device: no remote copies, remote signals or barrier semaphores. Data moves between devices by JAX's collectives and lax.ppermute only.
A program may use at most 128 MiB of HBM per device.

v0:
```python
import jax
import jax.numpy as jnp
from jax import lax
from jax.sharding import PartitionSpec as P

BLOCK = 16
TILE = 128
ITERS = 4


sphere_radius = 1.2
band_limit = 3.0
theta_floor = 0.2
jacobi_weight = 2.0 / 3.0


def padded_2(block, sides, width):
    for axis, dim in sides:
        count = lax.axis_size(axis)
        forward = [(i, i + 1) for i in range(count - 1)]
        backward = [(target, source) for source, target in forward]
        low = lax.ppermute(
            lax.slice_in_dim(block, block.shape[dim] - width, None, axis=dim), axis, forward
        )
        high = lax.ppermute(lax.slice_in_dim(block, 0, width, axis=dim), axis, backward)
        block = jnp.concatenate([low, block, high], axis=dim)
    return block


def cell_centres(block_edge):
    flat_index = jnp.arange(block_edge**3, dtype=jnp.int32)
    along_x = (flat_index // (block_edge * block_edge)).astype(jnp.float32) + 0.5
    along_y = (flat_index // block_edge % block_edge).astype(jnp.float32) + 0.5
    along_z = (flat_index % block_edge).astype(jnp.float32) + 0.5
    return (along_x, along_y, along_z)


def splat_group(points, block_edge):
    along_x, along_y, along_z = cell_centres(block_edge)
    squared = (points[:, 0, :, None] - along_x) ** 2 + (points[:, 1, :, None] - along_y) ** 2
    squared = squared + (points[:, 2, :, None] - along_z) ** 2
    nearest = jnp.sqrt(jnp.min(squared, axis=1)) - sphere_radius
    return jnp.minimum(nearest, band_limit)


def splat_tiles(points, block_edge, group_size):
    count = points.shape[0]
    grouped = points.reshape(count // group_size, group_size, 3, points.shape[2])
    fields = lax.map(lambda group_points: splat_group(group_points, block_edge), grouped)
    return fields.reshape(count, block_edge**3)


def neighbours(padded):
    return [
        padded[2:, 1:-1, 1:-1],
        padded[:-2, 1:-1, 1:-1],
        padded[1:-1, 2:, 1:-1],
        padded[1:-1, :-2, 1:-1],
        padded[1:-1, 1:-1, 2:],
        padded[1:-1, 1:-1, :-2],
    ]


def coefficients(level_set, padded_level, padded_fluid, padded_inside):
    magnitude = jnp.abs(level_set)
    diagonal = jnp.zeros_like(level_set)
    weights = []
    for beside_level, beside_fluid, beside_inside in zip(
        neighbours(padded_level), neighbours(padded_fluid), neighbours(padded_inside)
    ):
        theta_ratio = jnp.maximum(
            magnitude / jnp.maximum(magnitude + jnp.abs(beside_level), 1.0), theta_floor
        )
        air_side = beside_inside * (1.0 - beside_fluid)
        diagonal = diagonal + beside_fluid + air_side / theta_ratio
        weights.append(beside_fluid)
    return (diagonal, weights)


def sweep_once(pressure, padded_pressure, weights, diagonal, divergence, fluid_cell):
    summed = divergence
    for weight, beside in zip(weights, neighbours(padded_pressure)):
        summed = summed + weight * beside
    return fluid_cell * ((1.0 - jacobi_weight) * pressure + jacobi_weight * summed / diagonal)


def edge_mask(length, place, count):
    position = jnp.arange(length + 2, dtype=jnp.int32)
    lower = (place > 0).astype(jnp.float32)
    upper = (place < count - 1).astype(jnp.float32)
    return jnp.where(position == 0, lower, jnp.where(position == length + 1, upper, 1.0))


def per_device(particle_pos, tile_dest, tile_block, fluid_flag, divergence):
    block_edge = BLOCK
    cell_count = block_edge**3
    rows_x, rows_y, depth_cells = divergence.shape
    along_gx = lax.axis_size("gx")
    along_gy = lax.axis_size("gy")
    bricks = along_gx * along_gy
    local_tiles = tile_dest.shape[0]
    slots = max(2, 2 * local_tiles // bricks)
    blocks_dev = rows_x // block_edge * (rows_y // block_edge) * (depth_cells // block_edge)
    points = particle_pos.reshape(3, local_tiles, TILE).transpose(1, 0, 2)
    target = tile_dest[:, 0]
    order_index = jnp.arange(local_tiles, dtype=jnp.int32)
    earlier = order_index[:, None] > order_index[None, :]
    same_owner = target[:, None] == target[None, :]
    slot_index = jnp.sum((earlier & same_owner).astype(jnp.int32), axis=1)
    position = target * slots + slot_index
    labels = jnp.full((bricks * slots,), blocks_dev, dtype=jnp.int32).at[position].set(tile_block)
    payload = splat_tiles(points, block_edge, 4)
    buffer = jnp.zeros((bricks * slots, payload.shape[1]), jnp.float32).at[position].set(payload)
    arrived, arrived_labels = (
        lax.all_to_all(
            buffer.reshape(bricks, slots, payload.shape[1]),
            ("gx", "gy"),
            split_axis=0,
            concat_axis=0,
            tiled=True,
        ),
        lax.all_to_all(
            labels.reshape(bricks, slots), ("gx", "gy"), split_axis=0, concat_axis=0, tiled=True
        ),
    )
    arrived = arrived.reshape(bricks * slots, payload.shape[1])
    arrived_labels = arrived_labels.reshape(bricks * slots)
    blocks = jnp.full((blocks_dev, cell_count), band_limit, dtype=jnp.float32)
    blocks = blocks.at[arrived_labels].min(arrived, mode="drop")
    level_set = blocks.reshape(
        rows_x // block_edge,
        rows_y // block_edge,
        depth_cells // block_edge,
        block_edge,
        block_edge,
        block_edge,
    )
    level_set = level_set.transpose(0, 3, 1, 4, 2, 5).reshape(rows_x, rows_y, depth_cells)
    fluid_cell = fluid_flag.astype(jnp.float32)
    stacked = jnp.stack([level_set, fluid_cell])
    rimmed = padded_2(stacked, (("gx", 1), ("gy", 2)), 1)
    rimmed = jnp.pad(rimmed, ((0, 0), (0, 0), (0, 0), (1, 1)))
    depth_mask = jnp.pad(jnp.ones((depth_cells,), jnp.float32), (1, 1))
    mask_x = edge_mask(rows_x, lax.axis_index("gx"), along_gx)
    mask_y = edge_mask(rows_y, lax.axis_index("gy"), along_gy)
    inside = mask_x[:, None, None] * mask_y[None, :, None] * depth_mask[None, None, :]
    diagonal, weights = coefficients(level_set, rimmed[0], rimmed[1], inside)
    pressure = jnp.zeros_like(level_set)
    for sweep_step in range(ITERS):
        padded = padded_2(pressure, (("gx", 0), ("gy", 1)), 1)
        padded = jnp.pad(padded, ((0, 0), (0, 0), (1, 1)))
        pressure = sweep_once(pressure, padded, weights, diagonal, divergence, fluid_cell)
    return (level_set, pressure)


def solution(mesh):
    placed = (
        P(None, ("gx", "gy")),
        P(("gx", "gy"), None),
        P(("gx", "gy")),
        P("gx", "gy", None),
        P("gx", "gy", None),
    )
    return jax.shard_map(
        per_device,
        mesh=mesh,
        in_specs=placed,
        out_specs=(P("gx", "gy", None), P("gx", "gy", None)),
        check_vma=False,
    )
```

profile of v0, /device:TPU:26, one launch (start us, length us, event | category | flops | bytes accessed | tf_op | source)
XLA Modules:
  0.0 438.1 jit_solution(11842541524474393405)
XLA Ops:
  4.1 10.3 %all-to-all-start = ((s32[128,1,2]{2,1,0:T(1,128)}), s32[128,1,2]{2,1,0:T(1,128)S(1)}, u32[]{:S(2)}, u32[]{:S(2)}) async-start(s32[128,1,2]{2,1,0:T(1,128)} %bitcast.8), calls=%async_computation | async-start | bytes 131072 | tf_op jit(solution)/shard_map/all_to_all | solution.py:122
  15.3 120.8 %while.13 = (s32[]{:T(128)}, f32[32,4,4096]{2,1,0:T(4,128)}, f32[32,4,3,128]{3,1,0,2:T(4,128)S(1)}, s32[]{:T(128)}) while((s32[]{:T(128)}, f32[32,4,4096]{2,1,0:T(4,128)}, f32[32,4,3,128]{3,1,0,2:T(4,128)S(1)}, s32[]{:T(128)}) %tuple.55), condition=%wide.region_4.5_spmd, body=%wide.region_2.4_spmd.sunk | while | flops 19042304 | bytes 325701 | solution.py:49
  15.4 3.1 add_reduce_fusion.2
  19.2 3.1 add_reduce_fusion.2
  22.9 3.1 add_reduce_fusion.2
  26.7 3.1 add_reduce_fusion.2
  30.5 3.1 add_reduce_fusion.2
  34.3 3.1 add_reduce_fusion.2
  38.0 3.1 add_reduce_fusion.2
  41.8 3.1 add_reduce_fusion.2
  45.6 3.1 add_reduce_fusion.2
  49.4 3.1 add_reduce_fusion.2
  53.1 3.1 add_reduce_fusion.2
  56.9 3.1 add_reduce_fusion.2
  60.7 3.1 add_reduce_fusion.2
  64.5 3.1 add_reduce_fusion.2
  79.6 3.1 add_reduce_fusion.2
  102.2 3.1 add_reduce_fusion.2
  128.6 3.1 add_reduce_fusion.2
  138.1 3.9 scatter_custom_fusion.1
  142.1 5.9 %reshape.187 = f32[128,2,4096]{2,1,0:T(2,128)} reshape(f32[256,4096]{1,0:T(8,128)} %scatter_custom_fusion.1) | data formatting | bytes 8388608 | tf_op jit(solution)/shard_map/reshape | solution.py:116
  148.0 10.2 %all-to-all-start.1 = ((f32[128,2,4096]{2,1,0:T(2,128)}), f32[128,2,4096]{2,1,0:T(2,128)}, u32[]{:S(2)}, u32[]{:S(2)}) async-start(f32[128,2,4096]{2,1,0:T(2,128)} %reshape.187), calls=%async_computation.1 | async-start | bytes 8388608 | tf_op jit(solution)/shard_map/all_to_all | solution.py:115
  158.2 5.4 %collective-permute-start.4 = (f32[1,64,256]{2,1,0:T(8,128)S(1)}, f32[1,64,256]{2,1,0:T(8,128)S(1)}, u32[]{:S(2)}, u32[]{:S(2)}) collective-permute-start(f32[1,64,256]{2,1,0:T(8,128)S(1)} %broadcast.349), channel_id=1, source_target_pairs={{8,0},{16,8},{24,16},{32,24},{40,32},{48,40},{56,48},{64,56},{72,6... | collective-permute-start | bytes 196616 | tf_op jit(solution)/shard_map/ppermute | solution.py:25
  169.2 40.0 %all-to-all-done.1 = f32[128,2,4096]{2,1,0:T(2,128)} async-done(((f32[128,2,4096]{2,1,0:T(2,128)}), f32[128,2,4096]{2,1,0:T(2,128)}, u32[]{:S(2)}, u32[]{:S(2)}) %all-to-all-start.1) | async-done | bytes 4194336 | tf_op jit(solution)/shard_map/all_to_all | solution.py:115
  209.2 6.2 %reshape.211 = f32[256,4096]{1,0:T(8,128)} reshape(f32[128,2,4096]{2,1,0:T(2,128)} %all-to-all-done.1) | data formatting | bytes 8388608 | tf_op jit(solution)/shard_map/reshape | solution.py:126
  215.4 9.1 %scatter_custom_fusion.2 = f32[128,4096]{1,0:T(8,128)} fusion(s32[256]{0:T(256)S(1)} %bitcast.48, f32[256,4096]{1,0:T(8,128)} %reshape.211, f32[]{:T(128)} %constant.146.clone.1), kind=kCustom, calls=%fused_computation.210 | custom fusion | flops 1048576 | bytes 2097664 | tf_op jit(solution)/shard_map/scatter-min | solution.py:129
  224.4 10.4 %reshape.189 = f32[2,4,16,16,16,16]{5,4,3,2,1,0:T(8,128)} reshape(f32[128,4096]{1,0:T(8,128)} %scatter_custom_fusion.2) | data formatting | bytes 4194304 | tf_op jit(solution)/shard_map/reshape | solution.py:130
  234.8 17.7 %copy.21 = f32[2,16,4,16,16,16]{5,4,3,2,1,0:T(8,128)} copy(f32[2,16,4,16,16,16]{5,3,1,4,2,0:T(8,128)} %bitcast.45) | data formatting | bytes 4194304 | tf_op jit(solution)/shard_map/transpose | solution.py:138
  252.5 12.5 %stack_reshape.3 = f32[1,32,64,256]{3,2,1,0:T(8,128)} reshape(f32[2,16,4,16,16,16]{5,4,3,2,1,0:T(8,128)} %copy.21) | data formatting | bytes 4194304 | tf_op jit(solution)/shard_map/stack;reshape | solution.py:140
  265.9 4.1 collective-permute-start.1
  279.2 3.3 collective-permute-start.3
  284.7 4.4 %select_maximum_fusion.17 = f32[34,66,258]{2,1,0:T(8,128)} fusion(f32[34,1,256]{2,1,0:T(1,128)S(1)} %collective-permute-done.6, f32[34,1,256]{2,1,0:T(1,128)S(1)} %collective-permute-done.7, f32[1,64,256]{2,1,0:T(8,128)S(1)} %collective-permute-done.4, f32[32,64,256]{2,1,0:T(8,128)S(1)} %broadcast_in_dim.55, f32[1,64,256]{2,1,0:T(8,128)S(1)} %collective-permute-done.5), kind=kLoop, calls=%fused_computation.57 | loop fusion | flops 6947424 | bytes 4613664 | tf_op jit(solution)/shard_map/concatenate | solution.py:26
  289.1 12.5 %reshape.190 = f32[32,64,256]{2,1,0:T(8,128)} reshape(f32[2,16,4,16,16,16]{5,4,3,2,1,0:T(8,128)} %copy.21) | data formatting | bytes 4194304 | tf_op jit(solution)/shard_map/reshape | solution.py:138
  301.6 8.7 %select_maximum_fusion = f32[2,34,66,258]{3,2,1,0:T(8,128)S(1)} fusion(f32[2,34,1,256]{3,2,1,0:T(1,128)S(1)} %collective-permute-done.3, f32[2,34,1,256]{3,2,1,0:T(1,128)S(1)} %collective-permute-done.2, f32[2,1,64,256]{3,2,1,0:T(8,128)S(1)} %collective-permute-done.1, f32[2,1,64,256]{3,2,1,0:T(8,128)S(1)} %collective-permute-done, ...), kind=kLoop, calls=%fused_computation.36 | loop fusion | flops 16210656 | bytes 9227328 | tf_op jit(solution)/shard_map/concatenate | solution.py:26
  312.4 19.5 %fusion.25 = (f32[32,64,256]{2,1,0:T(8,128)}, f32[32,64,256]{2,1,0:T(8,128)}) fusion(f32[32,64,256]{2,1,0:T(8,128)} %param.11, f32[1,64,256]{2,1,0:T(8,128)S(1)} %collective-permute-done.4, f32[1,64,256]{2,1,0:T(8,128)S(1)} %collective-permute-done.5, f32[34,66,258]{2,1,0:T(8,128)} %select_maximum_fusion.17, f32[34,1,256]{2,1,0:T(1,128)S(1)} %collective-permute-done.7, ...), kind=kLoop, calls=%fused_computation.74 | loop fusion | flops 42991616 | bytes 54726656 | tf_op jit(solution)/shard_map/mul | solution.py:84
  332.9 6.0 %collective-permute-start.8 = (f32[1,64,256]{2,1,0:T(8,128)S(1)}, f32[1,64,256]{2,1,0:T(8,128)S(1)}, u32[]{:S(2)}, u32[]{:S(2)}) collective-permute-start(f32[1,64,256]{2,1,0:T(8,128)S(1)} %get-tuple-element.106), channel_id=1, source_target_pairs={{8,0},{16,8},{24,16},{32,24},{40,32},{48,40},{56,48},{64,56},{72,6... | collective-permute-start | bytes 196616 | tf_op jit(solution)/shard_map/ppermute | solution.py:25
  340.9 6.3 %collective-permute-done.9 = f32[1,64,256]{2,1,0:T(8,128)S(1)} collective-permute-done((f32[1,64,256]{2,1,0:T(8,128)S(1)}, f32[1,64,256]{2,1,0:T(8,128)S(1)}, u32[]{:S(2)}, u32[]{:S(2)}) %collective-permute-start.9) | collective-permute-done | bytes 65568 | tf_op jit(solution)/shard_map/ppermute | solution.py:22
  353.6 3.1 collective-permute-done.11
  356.6 4.4 %select_maximum_fusion.13 = f32[34,66,258]{2,1,0:T(8,128)} fusion(f32[34,1,256]{2,1,0:T(1,128)S(1)} %collective-permute-done.10, f32[34,1,256]{2,1,0:T(1,128)S(1)} %collective-permute-done.11, f32[1,64,256]{2,1,0:T(8,128)S(1)} %collective-permute-done.8, f32[32,64,256]{2,1,0:T(8,128)S(1)} %copy-done.2, f32[1,64,256]{2,1,0:T(8,128)S(1)} %collective-permute-done.9), kind=kLoop, calls=%fused_computation.52 | loop fusion | flops 6947424 | bytes 4613664 | tf_op jit(solution)/shard_map/concatenate | solution.py:26
  361.1 10.7 %fusion.59 = f32[32,64,256]{2,1,0:T(8,128)S(1)} fusion(f32[32,64,256]{2,1,0:T(8,128)} %get-tuple-element.81, f32[34,66,258]{2,1,0:T(8,128)} %select_maximum_fusion.13, f32[34,1,256]{2,1,0:T(1,128)S(1)} %collective-permute-done.11, f32[1,64,256]{2,1,0:T(8,128)S(1)} %collective-permute-done.8, f32[32,64,256]{2,1,0:T(8,128)S(1)} %copy-done.2, ...), kind=kLoop, calls=%fused_computation.129 | loop fusion | flops 13631488 | bytes 27463680 | tf_op jit(solution)/shard_map/mul | solution.py:84
  373.7 3.9 collective-permute-start.13
  377.9 4.0 collective-permute-done.13
  389.2 4.4 %select_maximum_fusion.9 = f32[34,66,258]{2,1,0:T(8,128)} fusion(f32[34,1,256]{2,1,0:T(1,128)S(1)} %collective-permute-done.14, f32[34,1,256]{2,1,0:T(1,128)S(1)} %collective-permute-done.15, f32[1,64,256]{2,1,0:T(8,128)S(1)} %collective-permute-done.12, f32[32,64,256]{2,1,0:T(8,128)S(1)} %fusion.59, f32[1,64,256]{2,1,0:T(8,128)S(1)} %collective-permute-done.13), kind=kLoop, calls=%fused_computation.48 | loop fusion | flops 6947424 | bytes 4613664 | tf_op jit(solution)/shard_map/concatenate | solution.py:26
  393.6 10.7 %fusion.45 = f32[32,64,256]{2,1,0:T(8,128)S(1)} fusion(f32[32,64,256]{2,1,0:T(8,128)} %get-tuple-element.81, f32[34,66,258]{2,1,0:T(8,128)} %select_maximum_fusion.9, f32[34,1,256]{2,1,0:T(1,128)S(1)} %collective-permute-done.15, f32[1,64,256]{2,1,0:T(8,128)S(1)} %collective-permute-done.12, f32[32,64,256]{2,1,0:T(8,128)S(1)} %fusion.59, ...), kind=kLoop, calls=%fused_computation.105 | loop fusion | flops 13631488 | bytes 27463680 | tf_op jit(solution)/shard_map/mul | solution.py:84
  406.2 3.9 collective-permute-start.17
  410.4 4.0 collective-permute-done.17
  421.9 4.4 %select_maximum_fusion.5 = f32[34,66,258]{2,1,0:T(8,128)} fusion(f32[34,1,256]{2,1,0:T(1,128)S(1)} %collective-permute-done.18, f32[34,1,256]{2,1,0:T(1,128)S(1)} %collective-permute-done.19, f32[1,64,256]{2,1,0:T(8,128)S(1)} %collective-permute-done.16, f32[32,64,256]{2,1,0:T(8,128)S(1)} %fusion.45, f32[1,64,256]{2,1,0:T(8,128)S(1)} %collective-permute-done.17), kind=kLoop, calls=%fused_computation.44 | loop fusion | flops 6947424 | bytes 4613664 | tf_op jit(solution)/shard_map/concatenate | solution.py:26
  426.3 11.3 %fusion.31 = f32[32,64,256]{2,1,0:T(8,128)} fusion(f32[32,64,256]{2,1,0:T(8,128)} %get-tuple-element.81, f32[34,66,258]{2,1,0:T(8,128)} %select_maximum_fusion.5, f32[34,1,256]{2,1,0:T(1,128)S(1)} %collective-permute-done.19, f32[1,64,256]{2,1,0:T(8,128)S(1)} %collective-permute-done.16, f32[32,64,256]{2,1,0:T(8,128)S(1)} %fusion.45, ...), kind=kLoop, calls=%fused_computation.81 | loop fusion | flops 13631488 | bytes 27463680 | tf_op jit(solution)/shard_map/mul | solution.py:84
  (250 shorter events, 122.9 us)
Async XLA Ops:
  4.1 143.9 %all-to-all-start = ((s32[128,1,2]{2,1,0:T(1,128)}), s32[128,1,2]{2,1,0:T(1,128)S(1)}, u32[]{:S(2)}, u32[]{:S(2)}) async-start(s32[128,1,2]{2,1,0:T(1,128)} %bitcast.8), calls=%async_computation | async-start | bytes 131072 | tf_op jit(solution)/shard_map/all_to_all | solution.py:122
  148.0 18.3 %copy-start.1 = (s32[32,64,256]{2,1,0:T(8,128)S(1)}, s32[32,64,256]{2,1,0:T(8,128)}, u32[]{:S(2)}) copy-start(s32[32,64,256]{2,1,0:T(8,128)} %param.10) | copy-start | bytes 6291460
  148.0 61.2 %all-to-all-start.1 = ((f32[128,2,4096]{2,1,0:T(2,128)}), f32[128,2,4096]{2,1,0:T(2,128)}, u32[]{:S(2)}, u32[]{:S(2)}) async-start(f32[128,2,4096]{2,1,0:T(2,128)} %reshape.187), calls=%async_computation.1 | async-start | bytes 8388608 | tf_op jit(solution)/shard_map/all_to_all | solution.py:115
  158.2 115.9 %collective-permute-start.4 = (f32[1,64,256]{2,1,0:T(8,128)S(1)}, f32[1,64,256]{2,1,0:T(8,128)S(1)}, u32[]{:S(2)}, u32[]{:S(2)}) collective-permute-start(f32[1,64,256]{2,1,0:T(8,128)S(1)} %broadcast.349), channel_id=1, source_target_pairs={{8,0},{16,8},{24,16},{32,24},{40,32},{48,40},{56,48},{64,56},{72,6... | collective-permute-start | bytes 196616 | tf_op jit(solution)/shard_map/ppermute | solution.py:25
  163.6 110.6 %collective-permute-start.5 = (f32[1,64,256]{2,1,0:T(8,128)S(1)}, f32[1,64,256]{2,1,0:T(8,128)S(1)}, u32[]{:S(2)}, u32[]{:S(2)}) collective-permute-start(f32[1,64,256]{2,1,0:T(8,128)S(1)} %broadcast.349), channel_id=1, source_target_pairs={{0,8},{8,16},{16,24},{24,32},{32,40},{40,48},{48,56},{56,64},{64,7... | collective-permute-start | bytes 196616 | tf_op jit(solution)/shard_map/ppermute | solution.py:22
  265.9 13.1 %collective-permute-start.1 = (f32[2,1,64,256]{3,2,1,0:T(8,128)S(1)}, f32[2,1,64,256]{3,2,1,0:T(8,128)S(1)}, u32[]{:S(2)}, u32[]{:S(2)}) collective-permute-start(f32[2,1,64,256]{3,2,1,0:T(8,128)S(1)} %get-tuple-element.92), channel_id=1, source_target_pairs={{8,0},{16,8},{24,16},{32,24},{40,32},{48,40},{56,48},{64,56},{72,6... | collective-permute-start | bytes 393224 | tf_op jit(solution)/shard_map/ppermute | solution.py:25
  270.0 9.1 %collective-permute-start = (f32[2,1,64,256]{3,2,1,0:T(8,128)S(1)}, f32[2,1,64,256]{3,2,1,0:T(8,128)S(1)}, u32[]{:S(2)}, u32[]{:S(2)}) collective-permute-start(f32[2,1,64,256]{3,2,1,0:T(8,128)S(1)} %get-tuple-element.91), channel_id=1, source_target_pairs={{0,8},{8,16},{16,24},{24,32},{32,40},{40,48},{48,56},{56,64},{64,7... | collective-permute-start | bytes 393224 | tf_op jit(solution)/shard_map/ppermute | solution.py:22
  274.2 4.9 %copy-start.5 = (f32[1,32,64,256]{3,2,1,0:T(8,128)S(1)}, f32[1,32,64,256]{3,2,1,0:T(8,128)}, u32[]{:S(2)}) copy-start(f32[1,32,64,256]{3,2,1,0:T(8,128)} %convert_bitcast_fusion) | copy-start | bytes 6291460
  274.2 5.0 %copy-start.6 = (f32[1,32,64,256]{3,2,1,0:T(8,128)S(1)}, f32[1,32,64,256]{3,2,1,0:T(8,128)}, u32[]{:S(2)}) copy-start(f32[1,32,64,256]{3,2,1,0:T(8,128)} %stack_reshape.3) | copy-start | bytes 6291460
  274.4 10.3 %copy-start.4 = (f32[32,64,256]{2,1,0:T(8,128)}, f32[32,64,256]{2,1,0:T(8,128)S(1)}, u32[]{:S(2)}) copy-start(f32[32,64,256]{2,1,0:T(8,128)S(1)} %broadcast_in_dim.55) | copy-start | bytes 6291460
  274.5 10.2 %collective-permute-start.6 = (f32[34,1,256]{2,1,0:T(1,128)S(1)}, f32[34,1,256]{2,1,0:T(1,128)S(1)}, u32[]{:S(2)}, u32[]{:S(2)}) collective-permute-start(f32[34,1,256]{2,1,0:T(1,128)S(1)} %get-tuple-element.100), channel_id=1, source_target_pairs={{1,0},{2,1},{3,2},{4,3},{5,4},{6,5},{7,6},{9,8},{10,9},{11,10},{12... | collective-permute-start | bytes 104456 | tf_op jit(solution)/shard_map/ppermute | solution.py:25
  276.8 7.9 %collective-permute-start.7 = (f32[34,1,256]{2,1,0:T(1,128)S(1)}, f32[34,1,256]{2,1,0:T(1,128)S(1)}, u32[]{:S(2)}, u32[]{:S(2)}) collective-permute-start(f32[34,1,256]{2,1,0:T(1,128)S(1)} %get-tuple-element.99), channel_id=1, source_target_pairs={{0,1},{1,2},{2,3},{3,4},{4,5},{5,6},{6,7},{8,9},{9,10},{10,11},{11... | collective-permute-start | bytes 104456 | tf_op jit(solution)/shard_map/ppermute | solution.py:22
  279.2 22.4 %collective-permute-start.3 = (f32[2,34,1,256]{3,2,1,0:T(1,128)S(1)}, f32[2,34,1,256]{3,2,1,0:T(1,128)S(1)}, u32[]{:S(2)}, u32[]{:S(2)}) collective-permute-start(f32[2,34,1,256]{3,2,1,0:T(1,128)S(1)} %get-tuple-element.90), channel_id=1, source_target_pairs={{1,0},{2,1},{3,2},{4,3},{5,4},{6,5},{7,6},{9,8},{10,9},{11,10},{12... | collective-permute-start | bytes 208904 | tf_op jit(solution)/shard_map/ppermute | solution.py:25
  282.5 19.1 %collective-permute-start.2 = (f32[2,34,1,256]{3,2,1,0:T(1,128)S(1)}, f32[2,34,1,256]{3,2,1,0:T(1,128)S(1)}, u32[]{:S(2)}, u32[]{:S(2)}) collective-permute-start(f32[2,34,1,256]{3,2,1,0:T(1,128)S(1)} %get-tuple-element.89), channel_id=1, source_target_pairs={{0,1},{1,2},{2,3},{3,4},{4,5},{5,6},{6,7},{8,9},{9,10},{10,11},{11... | collective-permute-start | bytes 208904 | tf_op jit(solution)/shard_map/ppermute | solution.py:22
  310.4 2.1 copy-start
  331.9 24.7 %copy-start.2 = (f32[32,64,256]{2,1,0:T(8,128)S(1)}, f32[32,64,256]{2,1,0:T(8,128)}, u32[]{:S(2)}) copy-start(f32[32,64,256]{2,1,0:T(8,128)} %get-tuple-element.80) | copy-start | bytes 6291460
  332.9 8.0 %collective-permute-start.8 = (f32[1,64,256]{2,1,0:T(8,128)S(1)}, f32[1,64,256]{2,1,0:T(8,128)S(1)}, u32[]{:S(2)}, u32[]{:S(2)}) collective-permute-start(f32[1,64,256]{2,1,0:T(8,128)S(1)} %get-tuple-element.106), channel_id=1, source_target_pairs={{8,0},{16,8},{24,16},{32,24},{40,32},{48,40},{56,48},{64,56},{72,6... | collective-permute-start | bytes 196616 | tf_op jit(solution)/shard_map/ppermute | solution.py:25
  339.0 8.3 %collective-permute-start.9 = (f32[1,64,256]{2,1,0:T(8,128)S(1)}, f32[1,64,256]{2,1,0:T(8,128)S(1)}, u32[]{:S(2)}, u32[]{:S(2)}) collective-permute-start(f32[1,64,256]{2,1,0:T(8,128)S(1)} %get-tuple-element.105), channel_id=1, source_target_pairs={{0,8},{8,16},{16,24},{24,32},{32,40},{40,48},{48,56},{56,64},{64,7... | collective-permute-start | bytes 196616 | tf_op jit(solution)/shard_map/ppermute | solution.py:22
  348.3 5.2 %collective-permute-start.10 = (f32[34,1,256]{2,1,0:T(1,128)S(1)}, f32[34,1,256]{2,1,0:T(1,128)S(1)}, u32[]{:S(2)}, u32[]{:S(2)}) collective-permute-start(f32[34,1,256]{2,1,0:T(1,128)S(1)} %get-tuple-element.98), channel_id=1, source_target_pairs={{1,0},{2,1},{3,2},{4,3},{5,4},{6,5},{7,6},{9,8},{10,9},{11,10},{12... | collective-permute-start | bytes 104456 | tf_op jit(solution)/shard_map/ppermute | solution.py:25
  351.4 5.3 %collective-permute-start.11 = (f32[34,1,256]{2,1,0:T(1,128)S(1)}, f32[34,1,256]{2,1,0:T(1,128)S(1)}, u32[]{:S(2)}, u32[]{:S(2)}) collective-permute-start(f32[34,1,256]{2,1,0:T(1,128)S(1)} %get-tuple-element.97), channel_id=1, source_target_pairs={{0,1},{1,2},{2,3},{3,4},{4,5},{5,6},{6,7},{8,9},{9,10},{10,11},{11... | collective-permute-start | bytes 104456 | tf_op jit(solution)/shard_map/ppermute | solution.py:22
  371.7 6.2 %collective-permute-start.12 = (f32[1,64,256]{2,1,0:T(8,128)S(1)}, f32[1,64,256]{2,1,0:T(8,128)S(1)}, u32[]{:S(2)}, u32[]{:S(2)}) collective-permute-start(f32[1,64,256]{2,1,0:T(8,128)S(1)} %get-tuple-element.104), channel_id=1, source_target_pairs={{8,0},{16,8},{24,16},{32,24},{40,32},{48,40},{56,48},{64,56},{72,6... | collective-permute-start | bytes 196616 | tf_op jit(solution)/shard_map/ppermute | solution.py:25
  373.7 8.3 %collective-permute-start.13 = (f32[1,64,256]{2,1,0:T(8,128)S(1)}, f32[1,64,256]{2,1,0:T(8,128)S(1)}, u32[]{:S(2)}, u32[]{:S(2)}) collective-permute-start(f32[1,64,256]{2,1,0:T(8,128)S(1)} %get-tuple-element.103), channel_id=1, source_target_pairs={{0,8},{8,16},{16,24},{24,32},{32,40},{40,48},{48,56},{56,64},{64,7... | collective-permute-start | bytes 196616 | tf_op jit(solution)/shard_map/ppermute | solution.py:22
  382.0 4.3 collective-permute-start.14
  383.9 5.3 %collective-permute-start.15 = (f32[34,1,256]{2,1,0:T(1,128)S(1)}, f32[34,1,256]{2,1,0:T(1,128)S(1)}, u32[]{:S(2)}, u32[]{:S(2)}) collective-permute-start(f32[34,1,256]{2,1,0:T(1,128)S(1)} %get-tuple-element.95), channel_id=1, source_target_pairs={{0,1},{1,2},{2,3},{3,4},{4,5},{5,6},{6,7},{8,9},{9,10},{10,11},{11... | collective-permute-start | bytes 104456 | tf_op jit(solution)/shard_map/ppermute | solution.py:22
  404.3 6.2 %collective-permute-start.16 = (f32[1,64,256]{2,1,0:T(8,128)S(1)}, f32[1,64,256]{2,1,0:T(8,128)S(1)}, u32[]{:S(2)}, u32[]{:S(2)}) collective-permute-start(f32[1,64,256]{2,1,0:T(8,128)S(1)} %get-tuple-element.102), channel_id=1, source_target_pairs={{8,0},{16,8},{24,16},{32,24},{40,32},{48,40},{56,48},{64,56},{72,6... | collective-permute-start | bytes 196616 | tf_op jit(solution)/shard_map/ppermute | solution.py:25
  406.2 8.3 %collective-permute-start.17 = (f32[1,64,256]{2,1,0:T(8,128)S(1)}, f32[1,64,256]{2,1,0:T(8,128)S(1)}, u32[]{:S(2)}, u32[]{:S(2)}) collective-permute-start(f32[1,64,256]{2,1,0:T(8,128)S(1)} %get-tuple-element.101), channel_id=1, source_target_pairs={{0,8},{8,16},{16,24},{24,32},{32,40},{40,48},{48,56},{56,64},{64,7... | collective-permute-start | bytes 196616 | tf_op jit(solution)/shard_map/ppermute | solution.py:22
  414.5 4.8 %collective-permute-start.18 = (f32[34,1,256]{2,1,0:T(1,128)S(1)}, f32[34,1,256]{2,1,0:T(1,128)S(1)}, u32[]{:S(2)}, u32[]{:S(2)}) collective-permute-start(f32[34,1,256]{2,1,0:T(1,128)S(1)} %get-tuple-element.94), channel_id=1, source_target_pairs={{1,0},{2,1},{3,2},{4,3},{5,4},{6,5},{7,6},{9,8},{10,9},{11,10},{12... | collective-permute-start | bytes 104456 | tf_op jit(solution)/shard_map/ppermute | solution.py:25
  416.5 9.8 %copy-start.3 = (f32[32,64,256]{2,1,0:T(8,128)S(1)}, f32[32,64,256]{2,1,0:T(8,128)}, u32[]{:S(2)}) copy-start(f32[32,64,256]{2,1,0:T(8,128)} %param.11) | copy-start | bytes 6291460
  416.5 5.4 %collective-permute-start.19 = (f32[34,1,256]{2,1,0:T(1,128)S(1)}, f32[34,1,256]{2,1,0:T(1,128)S(1)}, u32[]{:S(2)}, u32[]{:S(2)}) collective-permute-start(f32[34,1,256]{2,1,0:T(1,128)S(1)} %get-tuple-element.93), channel_id=1, source_target_pairs={{0,1},{1,2},{2,3},{3,4},{4,5},{5,6},{6,7},{8,9},{9,10},{10,11},{11... | collective-permute-start | bytes 104456 | tf_op jit(solution)/shard_map/ppermute | solution.py:22
where the time goes:
time: 445 us; the launch traced here: 438 us
  other arithmetic  216 us (49%)
  local copies, waits for them, and re-layouts  78.2 us (18%)
  starting transfers between devices  78.2 us (18%)
  waiting for transfers between devices  63.5 us (14%)
    reduce_min x32, other arithmetic, splat_group(): nearest = jnp.sqrt(jnp.min(squared, axis=1)) - sphere_radius  97.8 us
    mul x4, other arithmetic, sweep_once(): fluid_cell * ((1.0 - jacobi_weight) * pressure + jacobi_weight * summed /...  52.1 us
    all_to_all x1, waiting for transfers between devices, per_device(): lax.all_to_all(buffer.reshape(bricks, slots, payload.shape[1]), ('gx', 'g...  40 us
    ppermute x10, starting transfers between devices, padded_2(): lax.ppermute(lax.slice_in_dim(block, 0, width, axis=dim), axis, backward)  31.8 us
    concatenate x9, other arithmetic, padded_2(): block = jnp.concatenate([low, block, high], axis=dim)  27.7 us
    ppermute x10, starting transfers between devices, padded_2(): lax.ppermute(lax.slice_in_dim(block, block.shape[dim] - width, None, axis...  25.9 us
    ppermute x10, waiting for transfers between devices, padded_2(): lax.ppermute(lax.slice_in_dim(block, block.shape[dim] - width, None, axis...  22.9 us
    dynamic_update_slice x32, other arithmetic, splat_tiles(): lax.map(lambda group_points: splat_group(group_points, block_edge), grouped)  21.8 us
  transfers between devices with their start and end apart: 22, of which 9 were waited for; matrix products, arithmetic and copies ran while one was open for 48% of the time, Pallas kernels for 0%

commit v1 on v0

v1 whole, which is shorter than its diff:
```python
import functools

import jax
import jax.numpy as jnp
from jax import lax
from jax.experimental import pallas as pl
from jax.experimental.pallas import tpu as pltpu
from jax.sharding import PartitionSpec as P

BLOCK = 16
TILE = 128
RADIUS = 1.2
BAND = 3.0
WEIGHT = 2.0 / 3.0
FAR = 1.0e9
HALO = 4
ROWS = 8

f32 = jnp.float32


def pack_kernel(dest_ref, block_ref, pos_ref, send_ref, count_ref):
    tiles = block_ref.shape[0]

    def clear(i, carry):
        count_ref[i] = 0
        return carry

    lax.fori_loop(0, count_ref.shape[0], clear, 0)
    send_ref[...] = jnp.full(send_ref.shape, -1.0, f32)

    def place(t, carry):
        owner = dest_ref[t]
        slot = count_ref[owner]
        count_ref[owner] = slot + 1
        row = owner * 2 + slot
        send_ref[row, 0:3, :] = pos_ref[:, pl.ds(pl.multiple_of(t * TILE, TILE), TILE)]
        send_ref[row, 3:4, :] = jnp.full((1, TILE), block_ref[t].astype(f32), f32)
        return carry

    lax.fori_loop(0, tiles, place, 0)


def splat_kernel(label_ref, spread_ref, rec_ref, out_ref, list_ref, part_ref, place_ref, dx_ref, dyz_ref, acc_ref, near_ref):
    records = label_ref.shape[0]

    def pick(i, n):
        @pl.when(label_ref[i] >= 0)
        def _():
            list_ref[n] = i

        return n + (label_ref[i] >= 0).astype(jnp.int32)

    count = lax.fori_loop(0, records, pick, jnp.int32(0))
    groups = (count + 7) // 8

    def fill(i, carry):
        list_ref[i] = list_ref[count - 1]
        return carry

    lax.fori_loop(count, groups * 8, fill, 0)

    near_ref[...] = jnp.full(near_ref.shape, FAR, f32)
    part_ref[96:128, :] = jnp.zeros((32, TILE), f32)
    cell = lax.broadcasted_iota(jnp.int32, (BLOCK, 128), 0).astype(f32) + 0.5
    lane = lax.broadcasted_iota(jnp.int32, (1, 128), 1)
    depth = (lane & 15).astype(f32) + 0.5

    def group(g, carry):
        for t in range(8):
            rec = rec_ref[list_ref[g * 8 + t]]
            part_ref[t * 4 : t * 4 + 4, :] = rec
        whole = part_ref[0:32, :]
        high = whole.astype(jnp.bfloat16).astype(f32)
        rest = whole - high
        middle = rest.astype(jnp.bfloat16).astype(f32)
        part_ref[0:32, :] = high
        part_ref[32:64, :] = middle
        part_ref[64:96, :] = rest - middle
        turned = jnp.transpose(part_ref[...], (1, 0)).astype(jnp.bfloat16)
        place_ref[...] = jnp.dot(turned, spread_ref[...], preferred_element_type=f32)

        def prepare(k, inner):
            for u in range(8):
                p = k * 8 + u
                row = place_ref[pl.ds(p, 1), :]
                dx = cell - row[:, 0:128]
                dy = cell - row[:, 128:256]
                dz = depth - row[:, 256:384]
                base = pl.multiple_of(p * BLOCK, BLOCK)
                dx_ref[pl.ds(base, BLOCK), :] = dx * dx
                dyz_ref[pl.ds(base, BLOCK), :] = dy * dy + dz * dz
            return inner

        lax.fori_loop(0, TILE // 8, prepare, 0)

        for quarter in range(4):

            def step(k, accs):
                accs = list(accs)
                for u in range(8):
                    base = pl.multiple_of((k * 8 + u) * BLOCK, BLOCK)
                    dyz = dyz_ref[pl.ds(base, BLOCK), :]
                    for i in range(4):
                        dx = dx_ref[pl.ds(base + (quarter * 4 + i), 1), :]
                        accs[i] = jnp.minimum(accs[i], dyz + dx)
                return tuple(accs)

            start = tuple(jnp.full((BLOCK, 128), FAR, f32) for _ in range(4))
            accs = lax.fori_loop(0, TILE // 8, step, start)
            for i in range(4):
                acc_ref[quarter * 4 + i] = accs[i]

        def merge(t, inner):
            label = label_ref[list_ref[g * 8 + t]]
            bx = label // 64
            by = (label // 16) % 4
            bz = label % 16
            half = bz // 8
            spot = bz % 8
            shift = ((spot - t) & 7) * 16
            mask = (lane >> 4) == spot
            xs = pl.ds(pl.multiple_of(bx * 16, 16), 16)
            ys = pl.ds(pl.multiple_of(by * 16, 16), 16)
            rolled = pltpu.roll(acc_ref[...].reshape(256, 128), shift, 1)
            rolled = jnp.where(mask, rolled, FAR).reshape(16, 16, 128)
            near_ref[half, xs, ys, :] = jnp.minimum(near_ref[half, xs, ys, :], rolled)
            return inner

        lax.fori_loop(0, 8, merge, 0)
        return carry

    lax.fori_loop(0, groups, group, 0)

    def finish(x, carry):
        for half in range(2):
            out_ref[x, :, half * 128 : half * 128 + 128] = jnp.minimum(jnp.sqrt(near_ref[half, x]) - RADIUS, BAND)
        return carry

    lax.fori_loop(0, out_ref.shape[0], finish, 0)


def inverse(a):
    r = pl.reciprocal(a, approx=True)
    r = r * (2.0 - a * r)
    return r * (2.0 - a * r)


def jacobi_kernel(level_ref, kind_ref, div_ref, lxl_ref, lxh_ref, kxl_ref, kxh_ref, dxl_ref, dxh_ref,
                  lyl_ref, lyh_ref, kyl_ref, kyh_ref, dyl_ref, dyh_ref, out_ref,
                  a_ref, u_ref, d_ref, c_ref, p_ref, q_ref, sem):
    nx, ny, nz = out_ref.shape
    H = HALO
    inner = pl.ds(ROWS, ny)
    copies = []
    for n, (mid, low, high, ext) in enumerate(
        ((level_ref, lxl_ref, lxh_ref, a_ref), (kind_ref, kxl_ref, kxh_ref, u_ref), (div_ref, dxl_ref, dxh_ref, d_ref))
    ):
        copies.append(pltpu.make_async_copy(mid, ext.at[pl.ds(H, nx), inner, :], sem.at[n, 0]))
        copies.append(pltpu.make_async_copy(low, ext.at[pl.ds(0, H), inner, :], sem.at[n, 1]))
        copies.append(pltpu.make_async_copy(high, ext.at[pl.ds(nx + H, H), inner, :], sem.at[n, 2]))
    for copy in copies:
        copy.start()
    zero = jnp.zeros((nx + 2 * H, ROWS, nz), f32)
    for low, high, ext in ((lyl_ref, lyh_ref, a_ref), (kyl_ref, kyh_ref, u_ref), (dyl_ref, dyh_ref, d_ref)):
        ext[:, 0:ROWS, :] = zero
        ext[:, ROWS + ny :, :] = zero
        ext[:, ROWS - H : ROWS, :] = low[...]
        ext[:, ROWS + ny : ROWS + ny + H, :] = high[...]
    for copy in copies:
        copy.wait()

    rows = ny + 2 * ROWS
    lane = lax.broadcasted_iota(jnp.int32, (rows, nz), 1)
    first = lane == 0
    last = lane == nz - 1

    def sides(v):
        return (
            jnp.where(first, 0.0, pltpu.roll(v, 1, 1)),
            jnp.where(last, 0.0, pltpu.roll(v, nz - 1, 1)),
            pltpu.roll(v, 1, 0),
            pltpu.roll(v, rows - 1, 0),
        )

    def coefficient(x, carry):
        a = jnp.abs(a_ref[x])
        u = u_ref[x]
        r = inverse(jnp.maximum(a, 1e-30))
        diagonal = None
        near_a = sides(a) + (jnp.abs(a_ref[x - 1]), jnp.abs(a_ref[x + 1]))
        near_u = sides(u) + (u_ref[x - 1], u_ref[x + 1])
        for b, w in zip(near_a, near_u):
            term = jnp.minimum(jnp.maximum(a + b, 1.0) * r, w)
            diagonal = term if diagonal is None else diagonal + term
        c = jnp.where(u == 1.0, WEIGHT * inverse(jnp.maximum(diagonal, 1.0)), 0.0)
        c_ref[x] = c
        p_ref[x] = c * d_ref[x]
        return carry

    lax.fori_loop(1, nx + 2 * H - 1, coefficient, 0)

    def around(ref, x):
        v = ref[x]
        down, up, left, right = sides(v)
        return v, (down + up) + (left + right) + (ref[x - 1] + ref[x + 1])

    def second(x, carry):
        v, total = around(p_ref, x)
        q_ref[x] = v * (4.0 / 3.0) + c_ref[x] * total
        return carry

    lax.fori_loop(2, nx + 2 * H - 2, second, 0)

    def third(x, carry):
        v, total = around(q_ref, x)
        d_ref[x] = v * (1.0 / 3.0) + p_ref[x] + c_ref[x] * total
        return carry

    lax.fori_loop(3, nx + 2 * H - 3, third, 0)

    def fourth(x, carry):
        v, total = around(d_ref, x)
        result = v * (1.0 / 3.0) + p_ref[x] + c_ref[x] * total
        out_ref[x - H] = result[ROWS : ROWS + ny, :]
        return carry

    lax.fori_loop(H, nx + H, fourth, 0)


def spread_matrix():
    row = jnp.arange(128)
    tile, coord = row % 32 // 4, row % 4
    column = jnp.arange(384)
    hit = (row[:, None] < 96) & (coord[:, None] == column[None, :] // 128)
    hit = hit & (tile[:, None] == column[None, :] % 128 // 16)
    return hit.astype(jnp.bfloat16)


def shifts(axis):
    count = lax.axis_size(axis)
    forward = [(i, i + 1) for i in range(count - 1)]
    return forward, [(j, i) for i, j in forward]


def swap(axis, low_part, high_part):
    forward, backward = shifts(axis)
    return lax.ppermute(high_part, axis, forward), lax.ppermute(low_part, axis, backward)


def halo(block):
    H = HALO
    xl, xh = swap("gx", block[:H], block[-H:])
    low = jnp.concatenate([xl[:, :H], block[:, :H], xh[:, :H]], axis=0)
    high = jnp.concatenate([xl[:, -H:], block[:, -H:], xh[:, -H:]], axis=0)
    yl, yh = swap("gy", low, high)
    return xl, xh, yl, yh


def per_device(particle_pos, tile_dest, tile_block, fluid_flag, divergence):
    nx, ny, nz = divergence.shape
    tiles = tile_block.shape[0]
    bricks = lax.axis_size("gx") * lax.axis_size("gy")
    smem = pl.BlockSpec(memory_space=pltpu.SMEM)
    vmem = pl.BlockSpec(memory_space=pltpu.VMEM)
    hbm = pl.BlockSpec(memory_space=pl.ANY)

    kind = 5.0 - 4.0 * fluid_flag.astype(f32)
    kxl, kxh, kyl, kyh = halo(kind)
    dxl, dxh, dyl, dyh = halo(divergence)

    send = pl.pallas_call(
        pack_kernel,
        out_shape=jax.ShapeDtypeStruct((bricks * 2, 4, TILE), f32),
        in_specs=[smem, smem, vmem],
        out_specs=vmem,
        scratch_shapes=[pltpu.SMEM((bricks,), jnp.int32)],
        compiler_params=pltpu.CompilerParams(vmem_limit_bytes=16 << 20),
        name="pack",
    )(tile_dest[:, 0], tile_block, particle_pos)
    arrived = lax.all_to_all(send, ("gx", "gy"), split_axis=0, concat_axis=0, tiled=True)
    labels = arrived[:, 3, 0].astype(jnp.int32)
    level = pl.pallas_call(
        splat_kernel,
        out_shape=jax.ShapeDtypeStruct((nx, ny, nz), f32),
        in_specs=[smem, vmem, vmem],
        out_specs=vmem,
        scratch_shapes=[
            pltpu.SMEM((bricks * 2 + 8,), jnp.int32),
            pltpu.VMEM((128, TILE), f32),
            pltpu.VMEM((TILE, 384), f32),
            pltpu.VMEM((TILE * BLOCK, 128), f32),
            pltpu.VMEM((TILE * BLOCK, 128), f32),
            pltpu.VMEM((BLOCK, BLOCK, 128), f32),
            pltpu.VMEM((2, nx, ny, 128), f32),
        ],
        compiler_params=pltpu.CompilerParams(vmem_limit_bytes=32 << 20),
        name="splat",
    )(labels, spread_matrix(), arrived)
    lxl, lxh, lyl, lyh = halo(level)
    ext = (nx + 2 * HALO, ny + 2 * ROWS, nz)
    pressure = pl.pallas_call(
        jacobi_kernel,
        out_shape=jax.ShapeDtypeStruct((nx, ny, nz), f32),
        in_specs=[hbm] * 9 + [vmem] * 6,
        out_specs=vmem,
        scratch_shapes=[pltpu.VMEM(ext, f32)] * 6 + [pltpu.SemaphoreType.DMA((3, 3))],
        compiler_params=pltpu.CompilerParams(vmem_limit_bytes=48 << 20),
        name="jacobi",
    )(level, kind, divergence, lxl, lxh, kxl, kxh, dxl, dxh, lyl, lyh, kyl, kyh, dyl, dyh)
    return (level, pressure)


def solution(mesh):
    placed = (
        P(None, ("gx", "gy")),
        P(("gx", "gy"), None),
        P(("gx", "gy")),
        P("gx", "gy", None),
        P("gx", "gy", None),
    )
    return jax.shard_map(
        per_device,
        mesh=mesh,
        in_specs=placed,
        out_specs=(P("gx", "gy", None), P("gx", "gy", None)),
        check_vma=False,
    )
```

time: 445 us -> 197 us (0.44)
  the two profiles are of different devices: /device:TPU:26 before, /device:TPU:13 now
where the time goes in v1:
time: 197 us; the launch traced here: 195 us
  starting transfers between devices  101 us (51%)
  Pallas kernels  74.4 us (38%)
  local copies, waits for them, and re-layouts  6.85 us (3%)
  waiting for transfers between devices  5.69 us (3%)
  other arithmetic  5.27 us (3%)
    ppermute x6, starting transfers between devices, swap(): lax.ppermute(high_part, axis, forward)  65.4 us
    pallas_call x1, Pallas kernels, per_device(): pl.pallas_call(splat_kernel, out_shape=jax.ShapeDtypeStruct((nx, ny, nz),...  45.5 us
    pallas_call x1, Pallas kernels, per_device(): pl.pallas_call(jacobi_kernel, out_shape=jax.ShapeDtypeStruct((nx, ny, nz)...  25.6 us
    ppermute x6, starting transfers between devices, swap(): lax.ppermute(low_part, axis, backward)  25.2 us
    all_to_all x1, starting transfers between devices, per_device(): lax.all_to_all(send, ('gx', 'gy'), split_axis=0, concat_axis=0, tiled=True)  10.7 us
    ppermute x6, waiting for transfers between devices, swap(): lax.ppermute(low_part, axis, backward)  4.96 us
    convert_element_type x1, other arithmetic, per_device(): labels = arrived[:, 3, 0].astype(jnp.int32)  4.62 us
  transfers between devices with their start and end apart: 13, of which 4 were waited for; matrix products, arithmetic and copies ran while one was open for 5% of the time, Pallas kernels for 23%

profile of v1, /device:TPU:13, one launch (start us, length us, event | category | flops | bytes accessed | tf_op | source)
XLA Modules:
  0.0 194.5 jit_solution(12586354871227528641)
XLA Ops:
  0.6 0.0 copy-start.1
  0.6 0.9 copy-done.1
  1.6 0.0 copy-start.2
  1.6 0.7 copy-done.2
  2.2 0.0 copy-start.3
  2.2 0.7 copy-done.3
  2.9 0.0 copy-start.5
  2.9 3.4 %pack.1 = f32[256,4,128]{2,1,0:T(4,128)} custom-call(s32[128]{0:T(128)S(1)} %bitcast.1, s32[128]{0:T(128)S(1)} %copy-done.3, f32[3,16384]{1,0:T(4,128)S(1)} %copy-done.1), custom_call_target="tpu_custom_call" | custom-call | tf_op jit(solution)/shard_map/pack/pallas_call | solution.py:272
  6.2 10.7 %all-to-all-start = ((f32[256,4,128]{2,1,0:T(4,128)}), f32[256,4,128]{2,1,0:T(4,128)S(1)}, u32[]{:S(2)}, u32[]{:S(2)}) async-start(f32[256,4,128]{2,1,0:T(4,128)} %pack.1), calls=%async_computation | async-start | bytes 1048576 | tf_op jit(solution)/shard_map/all_to_all | solution.py:281
  17.0 1.1 fusion.13
  18.0 5.0 %collective-permute-start.5 = (f32[4,64,256]{2,1,0:T(8,128)S(1)}, f32[4,64,256]{2,1,0:T(8,128)S(1)}, u32[]{:S(2)}, u32[]{:S(2)}) collective-permute-start(f32[4,64,256]{2,1,0:T(8,128)S(1)} %get-tuple-element.8), channel_id=1, source_target_pairs={{8,0},{16,8},{24,16},{32,24},{40,32},{48,40},{56,48},{64,56},{72,6... | collective-permute-start | bytes 786440 | tf_op jit(solution)/shard_map/ppermute | solution.py:248
  23.1 1.9 collective-permute-start.4
  25.0 0.0 copy-done.5
  25.0 0.3 multiply_subtract_fusion.kind_ref
  25.3 0.0 copy-start.4
  25.4 5.5 %collective-permute-start.3 = (f32[4,64,256]{2,1,0:T(8,128)S(1)}, f32[4,64,256]{2,1,0:T(8,128)S(1)}, u32[]{:S(2)}, u32[]{:S(2)}) collective-permute-start(f32[4,64,256]{2,1,0:T(8,128)S(1)} %get-tuple-element.10), channel_id=1, source_target_pairs={{8,0},{16,8},{24,16},{32,24},{40,32},{48,40},{56,48},{64,56},{72,6... | collective-permute-start | bytes 786440 | tf_op jit(solution)/shard_map/ppermute | solution.py:248
  30.8 1.9 collective-permute-start.2
  32.8 1.1 fusion.10
  33.9 0.1 and_convert_fusion.spread_ref
  34.1 0.0 collective-permute-done.5.dxh_ref
  34.1 0.2 collective-permute-done.4.dxl_ref
  34.4 4.6 %collective-permute-start.10 = (f32[40,4,256]{2,1,0:T(4,128)S(1)}, f32[40,4,256]{2,1,0:T(4,128)S(1)}, u32[]{:S(2)}, u32[]{:S(2)}) collective-permute-start(f32[40,4,256]{2,1,0:T(4,128)S(1)} %pad_maximum_fusion.4), channel_id=1, source_target_pairs={{0,1},{1,2},{2,3},{3,4},{4,5},{5,6},{6,7},{8,9},{9,10},{10,11},{11... | collective-permute-start | bytes 491528 | tf_op jit(solution)/shard_map/ppermute | solution.py:248
  39.0 1.9 collective-permute-start.11
  40.9 0.0 collective-permute-done.3.kxh_ref
  40.9 0.5 collective-permute-done.2.kxl_ref
  41.5 0.0 copy-done.4
  41.5 5.2 %collective-permute-start.8 = (f32[40,4,256]{2,1,0:T(4,128)S(1)}, f32[40,4,256]{2,1,0:T(4,128)S(1)}, u32[]{:S(2)}, u32[]{:S(2)}) collective-permute-start(f32[40,4,256]{2,1,0:T(4,128)S(1)} %pad_maximum_fusion.2), channel_id=1, source_target_pairs={{0,1},{1,2},{2,3},{3,4},{4,5},{5,6},{6,7},{8,9},{9,10},{10,11},{11... | collective-permute-start | bytes 491528 | tf_op jit(solution)/shard_map/ppermute | solution.py:248
  46.7 0.0 all-to-all-done.rec_ref
  46.7 4.6 %fusion.label_ref = s32[256]{0:T(256)S(1)} fusion(f32[256,4,128]{2,1,0:T(4,128)S(1)} %all-to-all-done.rec_ref), kind=kLoop, calls=%fused_computation.9 | loop fusion | flops 256 | bytes 2048 | tf_op jit(solution)/shard_map/convert_element_type | solution.py:282
  51.3 45.5 %splat.1.level_ref = f32[32,64,256]{2,1,0:T(8,128)} custom-call(s32[256]{0:T(256)S(1)} %fusion.label_ref, bf16[128,384]{1,0:T(8,128)(2,1)S(1)} %and_convert_fusion.spread_ref, f32[256,4,128]{2,1,0:T(4,128)S(1)} %all-to-all-done.rec_ref), custom_call_target="tpu_custom_call" | custom-call | tf_op jit(solution)/shard_map/splat/pallas_call | solution.py:283
  96.8 0.0 copy-start
  96.8 1.2 fusion.15
  98.1 3.2 %collective-permute-start.1 = (f32[4,64,256]{2,1,0:T(8,128)S(1)}, f32[4,64,256]{2,1,0:T(8,128)S(1)}, u32[]{:S(2)}, u32[]{:S(2)}) collective-permute-start(f32[4,64,256]{2,1,0:T(8,128)S(1)} %get-tuple-element.12), channel_id=1, source_target_pairs={{8,0},{16,8},{24,16},{32,24},{40,32},{48,40},{56,48},{64,56},{72,6... | collective-permute-start | bytes 786440 | tf_op jit(solution)/shard_map/ppermute | solution.py:248
  101.3 49.9 %collective-permute-start = (f32[4,64,256]{2,1,0:T(8,128)S(1)}, f32[4,64,256]{2,1,0:T(8,128)S(1)}, u32[]{:S(2)}, u32[]{:S(2)}) collective-permute-start(f32[4,64,256]{2,1,0:T(8,128)S(1)} %get-tuple-element.13), channel_id=1, source_target_pairs={{0,8},{8,16},{16,24},{24,32},{32,40},{40,48},{48,56},{56,64},{64,7... | collective-permute-start | bytes 786440 | tf_op jit(solution)/shard_map/ppermute | solution.py:248
  151.3 1.1 fusion.12
  152.3 0.7 collective-permute-done.1.lxh_ref
  153.0 5.5 %collective-permute-start.9 = (f32[40,4,256]{2,1,0:T(4,128)S(1)}, f32[40,4,256]{2,1,0:T(4,128)S(1)}, u32[]{:S(2)}, u32[]{:S(2)}) collective-permute-start(f32[40,4,256]{2,1,0:T(4,128)S(1)} %pad_maximum_fusion.3), channel_id=1, source_target_pairs={{1,0},{2,1},{3,2},{4,3},{5,4},{6,5},{7,6},{9,8},{10,9},{11,10},{12... | collective-permute-start | bytes 491528 | tf_op jit(solution)/shard_map/ppermute | solution.py:248
  158.5 0.0 collective-permute-done.lxl_ref
  158.6 1.9 collective-permute-start.6
  160.6 0.0 collective-permute-done.10.dyl_ref
  160.6 4.1 %collective-permute-start.7 = (f32[40,4,256]{2,1,0:T(4,128)S(1)}, f32[40,4,256]{2,1,0:T(4,128)S(1)}, u32[]{:S(2)}, u32[]{:S(2)}) collective-permute-start(f32[40,4,256]{2,1,0:T(4,128)S(1)} %pad_maximum_fusion.1), channel_id=1, source_target_pairs={{1,0},{2,1},{3,2},{4,3},{5,4},{6,5},{7,6},{9,8},{10,9},{11,10},{12... | collective-permute-start | bytes 491528 | tf_op jit(solution)/shard_map/ppermute | solution.py:248
  164.7 0.0 collective-permute-done.11.dyh_ref
  164.7 0.0 collective-permute-done.8.kyl_ref
  164.7 0.0 collective-permute-done.9.kyh_ref
  164.7 0.0 collective-permute-done.6.lyl_ref
  164.7 4.3 %collective-permute-done.7.lyh_ref = f32[40,4,256]{2,1,0:T(4,128)S(1)} collective-permute-done((f32[40,4,256]{2,1,0:T(4,128)S(1)}, f32[40,4,256]{2,1,0:T(4,128)S(1)}, u32[]{:S(2)}, u32[]{:S(2)}) %collective-permute-start.7) | collective-permute-done | bytes 163872 | tf_op jit(solution)/shard_map/ppermute | solution.py:248
  169.0 0.0 copy-done
  169.0 25.6 %jacobi.1 = f32[32,64,256]{2,1,0:T(8,128)} custom-call(f32[32,64,256]{2,1,0:T(8,128)S(1)} %copy-done, f32[32,64,256]{2,1,0:T(8,128)} %copy-done.4, f32[32,64,256]{2,1,0:T(8,128)} %div_ref.1, f32[4,64,256]{2,1,0:T(8,128)S(1)} %collective-permute-done.lxl_ref, f32[4,64,256]{2,1,0:T(8,128)S(1)} %collective-permute-done.1.lxh_ref, ...), custom_call_target="tpu_custom_call" | custom-call | tf_op jit(solution)/shard_map/jacobi/pallas_call | solution.py:302
  (17 shorter events, 0.4 us)
Async XLA Ops:
  0.6 1.0 copy-start.1
  1.6 0.7 copy-start.2
  2.2 0.7 copy-start.3
  2.9 22.1 %copy-start.5 = (s32[32,64,256]{2,1,0:T(8,128)S(1)}, s32[32,64,256]{2,1,0:T(8,128)}, u32[]{:S(2)}) copy-start(s32[32,64,256]{2,1,0:T(8,128)} %param.8) | copy-start | bytes 6291460
  6.2 40.4 %all-to-all-start = ((f32[256,4,128]{2,1,0:T(4,128)}), f32[256,4,128]{2,1,0:T(4,128)S(1)}, u32[]{:S(2)}, u32[]{:S(2)}) async-start(f32[256,4,128]{2,1,0:T(4,128)} %pack.1), calls=%async_computation | async-start | bytes 1048576 | tf_op jit(solution)/shard_map/all_to_all | solution.py:281
  18.0 16.1 %collective-permute-start.5 = (f32[4,64,256]{2,1,0:T(8,128)S(1)}, f32[4,64,256]{2,1,0:T(8,128)S(1)}, u32[]{:S(2)}, u32[]{:S(2)}) collective-permute-start(f32[4,64,256]{2,1,0:T(8,128)S(1)} %get-tuple-element.8), channel_id=1, source_target_pairs={{8,0},{16,8},{24,16},{32,24},{40,32},{48,40},{56,48},{64,56},{72,6... | collective-permute-start | bytes 786440 | tf_op jit(solution)/shard_map/ppermute | solution.py:248
  23.1 11.2 %collective-permute-start.4 = (f32[4,64,256]{2,1,0:T(8,128)S(1)}, f32[4,64,256]{2,1,0:T(8,128)S(1)}, u32[]{:S(2)}, u32[]{:S(2)}) collective-permute-start(f32[4,64,256]{2,1,0:T(8,128)S(1)} %get-tuple-element.9), channel_id=1, source_target_pairs={{0,8},{8,16},{16,24},{24,32},{32,40},{40,48},{48,56},{56,64},{64,7... | collective-permute-start | bytes 786440 | tf_op jit(solution)/shard_map/ppermute | solution.py:248
  25.3 16.2 %copy-start.4 = (f32[32,64,256]{2,1,0:T(8,128)}, f32[32,64,256]{2,1,0:T(8,128)S(1)}, u32[]{:S(2)}) copy-start(f32[32,64,256]{2,1,0:T(8,128)S(1)} %multiply_subtract_fusion.kind_ref) | copy-start | bytes 6291460
  25.4 15.5 %collective-permute-start.3 = (f32[4,64,256]{2,1,0:T(8,128)S(1)}, f32[4,64,256]{2,1,0:T(8,128)S(1)}, u32[]{:S(2)}, u32[]{:S(2)}) collective-permute-start(f32[4,64,256]{2,1,0:T(8,128)S(1)} %get-tuple-element.10), channel_id=1, source_target_pairs={{8,0},{16,8},{24,16},{32,24},{40,32},{48,40},{56,48},{64,56},{72,6... | collective-permute-start | bytes 786440 | tf_op jit(solution)/shard_map/ppermute | solution.py:248
  30.8 10.6 %collective-permute-start.2 = (f32[4,64,256]{2,1,0:T(8,128)S(1)}, f32[4,64,256]{2,1,0:T(8,128)S(1)}, u32[]{:S(2)}, u32[]{:S(2)}) collective-permute-start(f32[4,64,256]{2,1,0:T(8,128)S(1)} %get-tuple-element.11), channel_id=1, source_target_pairs={{0,8},{8,16},{16,24},{24,32},{32,40},{40,48},{48,56},{56,64},{64,7... | collective-permute-start | bytes 786440 | tf_op jit(solution)/shard_map/ppermute | solution.py:248
  34.4 126.2 %collective-permute-start.10 = (f32[40,4,256]{2,1,0:T(4,128)S(1)}, f32[40,4,256]{2,1,0:T(4,128)S(1)}, u32[]{:S(2)}, u32[]{:S(2)}) collective-permute-start(f32[40,4,256]{2,1,0:T(4,128)S(1)} %pad_maximum_fusion.4), channel_id=1, source_target_pairs={{0,1},{1,2},{2,3},{3,4},{4,5},{5,6},{6,7},{8,9},{9,10},{10,11},{11... | collective-permute-start | bytes 491528 | tf_op jit(solution)/shard_map/ppermute | solution.py:248
  39.0 125.7 %collective-permute-start.11 = (f32[40,4,256]{2,1,0:T(4,128)S(1)}, f32[40,4,256]{2,1,0:T(4,128)S(1)}, u32[]{:S(2)}, u32[]{:S(2)}) collective-permute-start(f32[40,4,256]{2,1,0:T(4,128)S(1)} %pad_maximum_fusion.5), channel_id=1, source_target_pairs={{1,0},{2,1},{3,2},{4,3},{5,4},{6,5},{7,6},{9,8},{10,9},{11,10},{12... | collective-permute-start | bytes 491528 | tf_op jit(solution)/shard_map/ppermute | solution.py:248
  41.5 123.2 %collective-permute-start.8 = (f32[40,4,256]{2,1,0:T(4,128)S(1)}, f32[40,4,256]{2,1,0:T(4,128)S(1)}, u32[]{:S(2)}, u32[]{:S(2)}) collective-permute-start(f32[40,4,256]{2,1,0:T(4,128)S(1)} %pad_maximum_fusion.2), channel_id=1, source_target_pairs={{0,1},{1,2},{2,3},{3,4},{4,5},{5,6},{6,7},{8,9},{9,10},{10,11},{11... | collective-permute-start | bytes 491528 | tf_op jit(solution)/shard_map/ppermute | solution.py:248
  96.8 72.1 %copy-start = (f32[32,64,256]{2,1,0:T(8,128)S(1)}, f32[32,64,256]{2,1,0:T(8,128)}, u32[]{:S(2)}) copy-start(f32[32,64,256]{2,1,0:T(8,128)} %splat.1.level_ref) | copy-start | bytes 6291460
  98.1 55.0 %collective-permute-start.1 = (f32[4,64,256]{2,1,0:T(8,128)S(1)}, f32[4,64,256]{2,1,0:T(8,128)S(1)}, u32[]{:S(2)}, u32[]{:S(2)}) collective-permute-start(f32[4,64,256]{2,1,0:T(8,128)S(1)} %get-tuple-element.12), channel_id=1, source_target_pairs={{8,0},{16,8},{24,16},{32,24},{40,32},{48,40},{56,48},{64,56},{72,6... | collective-permute-start | bytes 786440 | tf_op jit(solution)/shard_map/ppermute | solution.py:248
  101.3 57.2 %collective-permute-start = (f32[4,64,256]{2,1,0:T(8,128)S(1)}, f32[4,64,256]{2,1,0:T(8,128)S(1)}, u32[]{:S(2)}, u32[]{:S(2)}) collective-permute-start(f32[4,64,256]{2,1,0:T(8,128)S(1)} %get-tuple-element.13), channel_id=1, source_target_pairs={{0,8},{8,16},{16,24},{24,32},{32,40},{40,48},{48,56},{56,64},{64,7... | collective-permute-start | bytes 786440 | tf_op jit(solution)/shard_map/ppermute | solution.py:248
  153.0 11.6 %collective-permute-start.9 = (f32[40,4,256]{2,1,0:T(4,128)S(1)}, f32[40,4,256]{2,1,0:T(4,128)S(1)}, u32[]{:S(2)}, u32[]{:S(2)}) collective-permute-start(f32[40,4,256]{2,1,0:T(4,128)S(1)} %pad_maximum_fusion.3), channel_id=1, source_target_pairs={{1,0},{2,1},{3,2},{4,3},{5,4},{6,5},{7,6},{9,8},{10,9},{11,10},{12... | collective-permute-start | bytes 491528 | tf_op jit(solution)/shard_map/ppermute | solution.py:248
  158.6 6.1 %collective-permute-start.6 = (f32[40,4,256]{2,1,0:T(4,128)S(1)}, f32[40,4,256]{2,1,0:T(4,128)S(1)}, u32[]{:S(2)}, u32[]{:S(2)}) collective-permute-start(f32[40,4,256]{2,1,0:T(4,128)S(1)} %pad_maximum_fusion), channel_id=1, source_target_pairs={{0,1},{1,2},{2,3},{3,4},{4,5},{5,6},{6,7},{8,9},{9,10},{10,11},{11... | collective-permute-start | bytes 491528 | tf_op jit(solution)/shard_map/ppermute | solution.py:248
  160.6 8.4 %collective-permute-start.7 = (f32[40,4,256]{2,1,0:T(4,128)S(1)}, f32[40,4,256]{2,1,0:T(4,128)S(1)}, u32[]{:S(2)}, u32[]{:S(2)}) collective-permute-start(f32[40,4,256]{2,1,0:T(4,128)S(1)} %pad_maximum_fusion.1), channel_id=1, source_target_pairs={{1,0},{2,1},{3,2},{4,3},{5,4},{6,5},{7,6},{9,8},{10,9},{11,10},{12... | collective-permute-start | bytes 491528 | tf_op jit(solution)/shard_map/ppermute | solution.py:248

commit v2 on v1

v2 whole, which is shorter than its diff:
```python
import functools

import jax
import jax.numpy as jnp
from jax import lax
from jax.experimental import pallas as pl
from jax.experimental.pallas import tpu as pltpu
from jax.sharding import PartitionSpec as P

BLOCK = 16
TILE = 128
RADIUS = 1.2
BAND = 3.0
WEIGHT = 2.0 / 3.0
FAR = 1.0e9
HALO = 4
ROWS = 8
REACH = RADIUS + BAND + 1.0e-3
PAIRS = 8

f32 = jnp.float32


def ordered(keys, first, second):
    row = lax.broadcasted_iota(jnp.int32, (8, TILE), 0)
    data = [list(keys), list(first), list(second)]
    size = 2
    while size <= TILE:
        if size >= 16 and size < TILE:
            sign = jnp.where((row & (size // 16)) == 0, 1.0, -1.0).astype(f32)
        else:
            sign = None
        gap = size // 2
        while gap >= 1:
            if gap < 16:
                for v in range(16):
                    if v & gap:
                        continue
                    w = v | gap
                    a, b = data[0][v], data[0][w]
                    if sign is not None:
                        swap_now = a * sign > b * sign
                    elif size < 16 and v & size:
                        swap_now = a < b
                    else:
                        swap_now = a > b
                    for part in data:
                        a, b = part[v], part[w]
                        part[v] = jnp.where(swap_now, b, a)
                        part[w] = jnp.where(swap_now, a, b)
            else:
                e = gap // 16
                low = (row & e) == 0
                way = jnp.where(low, 1.0, -1.0).astype(f32)
                if sign is not None:
                    way = way * sign
                for v in range(16):
                    others = []
                    for part in data:
                        if e == 4:
                            others.append(pltpu.roll(part[v], 4, 0))
                        else:
                            others.append(jnp.where(low, pltpu.roll(part[v], 8 - e, 0), pltpu.roll(part[v], e, 0)))
                    take = data[0][v] * way > others[0] * way
                    for part, other in zip(data, others):
                        part[v] = jnp.where(take, other, part[v])
            gap //= 2
        size *= 2
    return data


def pack_kernel(dest_ref, block_ref, pos_ref, send_ref, count_ref, tile_ref, turn_ref):
    tiles = block_ref.shape[0]
    lane = lax.broadcasted_iota(jnp.int32, (4, TILE), 1)
    note = (lax.broadcasted_iota(jnp.int32, (4, TILE), 0) == 3) & (lane == 0)

    def clear(i, carry):
        count_ref[i] = 0
        return carry

    lax.fori_loop(0, count_ref.shape[0], clear, 0)
    empty = jnp.where(lane == 0, -1.0, jnp.where(lane <= PAIRS, float(TILE), 0.0)).astype(f32)
    send_ref[...] = jnp.broadcast_to(empty[None], send_ref.shape)

    for t in range(tiles):
        tile_ref[0:3, t, :] = pos_ref[:, t * TILE : t * TILE + TILE]
    parts = []
    for c in range(3):
        turned = jnp.transpose(tile_ref[c], (1, 0))
        parts.append([turned[v * 8 : v * 8 + 8, :] for v in range(16)])
    parts = ordered(*parts)
    turn_ref[3] = jnp.zeros((TILE, TILE), f32)
    for k in range(PAIRS):
        below = jnp.zeros((8, TILE), f32)
        upto = jnp.zeros((8, TILE), f32)
        for v in range(16):
            below = below + jnp.where(parts[0][v] < 2 * k + 0.5 - REACH, 1.0, 0.0)
            upto = upto + jnp.where(parts[0][v] < 2 * k + 1.5 + REACH, 1.0, 0.0)
        turn_ref[3, 1 + k : 2 + k, :] = jnp.sum(below, axis=0, keepdims=True)
        turn_ref[3, 1 + PAIRS + k : 2 + PAIRS + k, :] = -jnp.sum(upto, axis=0, keepdims=True)
    for c in range(3):
        for v in range(16):
            turn_ref[c, pl.ds(v, 8, stride=16), :] = parts[c][v]
    for c in range(4):
        tile_ref[c] = jnp.transpose(turn_ref[c], (1, 0))

    def place(t, carry):
        owner = dest_ref[t]
        slot = count_ref[owner]
        count_ref[owner] = slot + 1
        send_ref[owner * 2 + slot] = jnp.where(note, block_ref[t].astype(f32), tile_ref[:, t, :])
        return carry

    lax.fori_loop(0, tiles, place, 0)


def ones_where(condition):
    return jnp.where(condition, 1.0, 0.0).astype(jnp.bfloat16)


def arrange(notes, note_ref, slot_ref):
    records = notes.shape[0]
    halves = records // 128
    turned = [jnp.transpose(notes[h * 128 : h * 128 + 128, :], (1, 0))[0:1, :] for h in range(halves)]
    labels = jnp.concatenate(turned, axis=1)
    valid = labels >= 0.0
    spot = (labels.astype(jnp.int32) & 7).astype(f32)
    column = lax.broadcasted_iota(jnp.int32, (8, records), 0).astype(f32)
    member = jnp.where(valid & (column == spot), 1.0, 0.0)
    earlier = ones_where(
        lax.broadcasted_iota(jnp.int32, (records, records), 0) < lax.broadcasted_iota(jnp.int32, (records, records), 1)
    )
    before = jnp.dot(member.astype(jnp.bfloat16), earlier, preferred_element_type=f32)
    rank = jnp.sum(member * before, axis=0, keepdims=True)
    counts = jnp.sum(member, axis=1, keepdims=True)
    total = jnp.sum(counts, axis=0, keepdims=True)
    room = 8.0 * jnp.floor((total + 63.0) * (1.0 / 64.0))
    late = jnp.where(valid & (rank >= room), 1.0, 0.0)
    turn = jnp.dot(jnp.broadcast_to(late, (8, records)).astype(jnp.bfloat16), earlier, preferred_element_type=f32)[0:1]
    used = jnp.minimum(counts, room)
    free = room - used
    offsets = [jnp.zeros((1, 1), f32)]
    for t in range(7):
        offsets.append(offsets[-1] + free[t : t + 1])
    offset = jnp.concatenate(offsets, axis=0)
    chosen = (turn >= offset) & (turn < offset + free)
    moved = jnp.sum(jnp.where(chosen, (used + turn - offset) * 8.0 + column, 0.0), axis=0, keepdims=True)
    slots = jnp.where(valid, jnp.where(late > 0.0, moved, rank * 8.0 + spot), -1.0)
    for h in range(halves):
        part = jnp.broadcast_to(slots[:, h * 128 : h * 128 + 128], (128, 128))
        slot_ref[h * 128 : h * 128 + 128, :] = jnp.transpose(part, (1, 0))
    lane = lax.broadcasted_iota(jnp.int32, (records, 128), 1).astype(f32)
    raised = jnp.broadcast_to(jnp.where(valid, labels + 1.0, 0.0), (8, records)).astype(jnp.bfloat16)
    for h in range(halves):
        here = jnp.dot(raised, ones_where(slot_ref[...] == lane + 128.0 * h), preferred_element_type=f32)
        note_ref[h : h + 1, :] = (here[0:1] - 1.0).astype(jnp.int32)
    least = jnp.min(notes, axis=0, keepdims=True)
    note_ref[halves : halves + 1, :] = jnp.where(lane[0:1] == 0.0, total, least).astype(jnp.int32)


def splat_kernel(rec_ref, out_ref, low_ref, high_ref, meta_ref, sem,
                 note_ref, slot_ref, split_ref, px_ref, py_ref, pz_ref, dyz_ref, acc_ref, near_ref):
    records = rec_ref.shape[0]
    halves = records // 128
    groups = records // 8
    nx = out_ref.shape[0]

    arrange(rec_ref[:, 3, :], note_ref, slot_ref)
    copy = pltpu.make_async_copy(note_ref, meta_ref, sem)
    copy.start()
    near_ref[...] = jnp.full(near_ref.shape, FAR, f32)
    for c in range(3):
        for h in range(halves):
            whole = jnp.transpose(rec_ref[h * 128 : h * 128 + 128, c, :], (1, 0))
            high = whole.astype(jnp.bfloat16)
            rest = whole - high.astype(f32)
            middle = rest.astype(jnp.bfloat16)
            last = (rest - middle.astype(f32)).astype(jnp.bfloat16)
            for n, part in enumerate((high, middle, last)):
                at = n * records + h * 128
                split_ref[c * TILE : c * TILE + TILE, at : at + 128] = part
    copy.wait()
    batches = (meta_ref[halves, 0] + 63) // 64

    lane = lax.broadcasted_iota(jnp.int32, (8, 128), 1)
    depth = (lane & 15).astype(f32) + 0.5
    spots = lax.broadcasted_iota(jnp.int32, (1, 128), 1) >> 4
    tile_lane = (lax.broadcasted_iota(jnp.int32, (records, 128), 1) >> 4).astype(f32)

    def expand(q, carry):
        slot = slot_ref[...] - (q * 16).astype(f32)
        hit = jnp.concatenate([ones_where(slot == tile_lane), ones_where(slot == tile_lane + 8.0)], axis=1)
        place = jnp.dot(split_ref[...], jnp.concatenate([hit] * 3, axis=0), preferred_element_type=f32)
        for n in range(2):
            rows = pl.ds(q * 2 + n, TILE, stride=groups)
            lanes = slice(n * 128, n * 128 + 128)
            px_ref[rows, :] = place[0:TILE, lanes]
            py_ref[rows, :] = place[TILE : 2 * TILE, lanes]
            pz_ref[rows, :] = place[2 * TILE : 3 * TILE, lanes]
        return carry

    lax.fori_loop(0, batches * 4, expand, 0)

    def batch(g, carry):
        def prepare(k, inner):
            for u in range(2):
                p = k * 2 + u
                rows = pl.ds(pl.multiple_of(p * groups + g * 8, 8), 8)
                py = py_ref[rows, :]
                dz = depth - pz_ref[rows, :]
                dz = dz * dz
                for y in range(16):
                    dy = (y + 0.5) - py
                    dyz_ref[p * 16 + y] = dy * dy + dz
            return inner

        lax.fori_loop(0, TILE // 2, prepare, 0)

        for k in range(PAIRS):
            stop = -meta_ref[halves, 1 + PAIRS + k]
            steps = (stop - meta_ref[halves, 1 + k] + 7) // 8
            first = jnp.maximum(stop - steps * 8, 0)

            def step(i, accs):
                accs = list(accs)
                for u in range(4):
                    p = first + i * 8 + u * 2
                    away = []
                    for v in range(2):
                        px = px_ref[pl.ds(pl.multiple_of((p + v) * groups + g * 8, 8), 8), :]
                        d0 = (2 * k + 0.5) - px
                        d1 = (2 * k + 1.5) - px
                        away.append((d0 * d0, d1 * d1))
                    for y in range(16):
                        one = dyz_ref[p * 16 + y]
                        two = dyz_ref[p * 16 + 16 + y]
                        for x in range(2):
                            both = jnp.minimum(one + away[0][x], two + away[1][x])
                            accs[x * 16 + y] = jnp.minimum(accs[x * 16 + y], both)
                return tuple(accs)

            accs = lax.fori_loop(0, steps, step, tuple(jnp.full((8, 128), FAR, f32) for _ in range(32)))
            for i in range(32):
                acc_ref[(k * 32 + i) * 8 : (k * 32 + i) * 8 + 8, :] = accs[i]

        def put_down(s, t, move):
            label = meta_ref[g // 2, g % 2 * 64 + s * 8 + t]
            spot = label & 7
            wanted = (label >= 0) & ((spot == t) != move)
            mask = spots == jnp.where(wanted, spot, -1)
            label = jnp.maximum(label, 0)
            bx = label // 64
            ys = pl.ds(pl.multiple_of(label // 16 % 4 * 16, 16), 16)
            half = label // 8 % 2

            def update():
                for x in range(16):
                    tile = acc_ref[pl.ds(x * 128 + s, 16, stride=8), :]
                    if move:
                        tile = pltpu.roll(tile, ((spot - t) & 7) * 16, 1)
                    tile = jnp.where(mask, tile, FAR)
                    near_ref[half, bx * 16 + x, ys, :] = jnp.minimum(near_ref[half, bx * 16 + x, ys, :], tile)

            if move:
                pl.when(wanted)(update)
            else:
                update()

        def merge(t, inner):
            for s in range(8):
                put_down(s, t, False)
            return inner

        lax.fori_loop(0, 8, merge, 0)

        def merge_late(t, inner):
            for s in range(8):
                put_down(s, t, True)
            return inner

        lax.fori_loop(0, 8, merge_late, 0)
        return carry

    lax.fori_loop(0, batches, batch, 0)

    def finish(x, carry):
        for half in range(2):
            out_ref[x, :, half * 128 : half * 128 + 128] = jnp.minimum(jnp.sqrt(near_ref[half, x]) - RADIUS, BAND)
        return carry

    lax.fori_loop(0, nx, finish, 0)
    low_ref[...] = out_ref[0:HALO]
    high_ref[...] = out_ref[nx - HALO : nx]


def jacobi_kernel(level_ref, kind_ref, div_ref, lxl_ref, lxh_ref, ixl_ref, ixh_ref, lyl_ref, lyh_ref, iyl_ref, iyh_ref, out_ref,
                  a_ref, u_ref, d_ref, c_ref, p_ref, q_ref, sem):
    nx, ny, nz = out_ref.shape
    H = HALO
    R = ROWS
    copies = []
    for n, (mid, low, high, ext) in enumerate(
        (
            (kind_ref, ixl_ref.at[0], ixh_ref.at[0], u_ref),
            (div_ref, ixl_ref.at[1], ixh_ref.at[1], d_ref),
            (level_ref, lxl_ref, lxh_ref, a_ref),
        )
    ):
        for half in range(2):
            lanes = pl.ds(half * 128, 128)
            for m, (source, at, size) in enumerate(((mid, H, nx), (low, 0, H), (high, nx + H, H))):
                copies.append(
                    pltpu.make_async_copy(
                        source.at[:, :, lanes], ext.at[pl.ds(at, size), half, pl.ds(R, ny), :], sem.at[n, m, half]
                    )
                )
    for copy in copies:
        copy.start()
    for low, high, ext in ((lyl_ref, lyh_ref, a_ref), (iyl_ref.at[0], iyh_ref.at[0], u_ref), (iyl_ref.at[1], iyh_ref.at[1], d_ref)):
        for half in range(2):
            lanes = slice(half * 128, half * 128 + 128)
            ext[:, half, R - H : R, :] = low[:, :, lanes]
            ext[:, half, R + ny : R + ny + H, :] = high[:, :, lanes]
    for copy in copies:
        copy.wait()

    lane = lax.broadcasted_iota(jnp.int32, (8, 128), 1)

    def along(pair, rows):
        first = jnp.broadcast_to(lane[0:1] == 0, (rows, 128))
        last = jnp.broadcast_to(lane[0:1] == 127, (rows, 128))
        up = [pltpu.roll(v, 1, 1) for v in pair]
        down = [pltpu.roll(v, 127, 1) for v in pair]
        return (
            (jnp.where(first, 0.0, up[0]), jnp.where(last, down[1], down[0])),
            (jnp.where(first, up[0], up[1]), jnp.where(last, 0.0, down[1])),
        )

    def coefficient(x, carry):
        r0, rows = R - H, ny + 2 * H
        at = slice(r0, r0 + rows)
        mags = [jnp.abs(a_ref[x, h, at, :]) for h in range(2)]
        kinds = [u_ref[x, h, at, :] for h in range(2)]
        za, zu = along(mags, rows), along(kinds, rows)
        for h in range(2):
            a, u = mags[h], kinds[h]
            r = 1.0 / jnp.maximum(a, 1e-30)
            diagonal = None
            near = [(za[h][0], zu[h][0]), (za[h][1], zu[h][1])]
            for dx, dy in ((-1, 0), (1, 0), (0, -1), (0, 1)):
                beside = slice(r0 + dy, r0 + dy + rows)
                near.append((jnp.abs(a_ref[x + dx, h, beside, :]), u_ref[x + dx, h, beside, :]))
            for b, w in near:
                term = jnp.minimum(jnp.maximum(a + b, 1.0) * r, w)
                diagonal = term if diagonal is None else diagonal + term
            c = jnp.where(u == 1.0, WEIGHT / jnp.maximum(diagonal, 1.0), 0.0)
            c_ref[x, h, at, :] = c
            p_ref[x, h, at, :] = c * d_ref[x, h, at, :]
        return carry

    lax.fori_loop(1, nx + 2 * H - 1, coefficient, 0, unroll=2)

    def around(ref, x, r0, rows):
        pair = [ref[x, h, r0 : r0 + rows, :] for h in range(2)]
        z = along(pair, rows)
        totals = []
        for h in range(2):
            total = z[h][0] + z[h][1]
            total = total + (ref[x - 1, h, r0 : r0 + rows, :] + ref[x + 1, h, r0 : r0 + rows, :])
            total = total + (ref[x, h, r0 - 1 : r0 - 1 + rows, :] + ref[x, h, r0 + 1 : r0 + 1 + rows, :])
            totals.append(total)
        return pair, totals

    def second(x, carry):
        r0, rows = R - H, ny + 2 * H
        at = slice(r0, r0 + rows)
        own, total = around(p_ref, x, r0, rows)
        for h in range(2):
            q_ref[x, h, at, :] = own[h] * (4.0 / 3.0) + c_ref[x, h, at, :] * total[h]
        return carry

    lax.fori_loop(2, nx + 2 * H - 2, second, 0, unroll=8)

    def third(x, carry):
        r0, rows = R - H, ny + 2 * H
        at = slice(r0, r0 + rows)
        own, total = around(q_ref, x, r0, rows)
        for h in range(2):
            d_ref[x, h, at, :] = own[h] * (1.0 / 3.0) + p_ref[x, h, at, :] + c_ref[x, h, at, :] * total[h]
        return carry

    lax.fori_loop(3, nx + 2 * H - 3, third, 0, unroll=8)

    def fourth(x, carry):
        at = slice(R, R + ny)
        own, total = around(d_ref, x, R, ny)
        for h in range(2):
            out_ref[x - H, :, h * 128 : h * 128 + 128] = (
                own[h] * (1.0 / 3.0) + p_ref[x, h, at, :] + c_ref[x, h, at, :] * total[h]
            )
        return carry

    lax.fori_loop(H, nx + H, fourth, 0, unroll=8)


def specs():
    return pl.BlockSpec(memory_space=pltpu.SMEM), pl.BlockSpec(memory_space=pltpu.VMEM), pl.BlockSpec(memory_space=pl.ANY)


def pack(dest, block, pos, bricks):
    smem, vmem, _ = specs()
    return pl.pallas_call(
        pack_kernel,
        out_shape=jax.ShapeDtypeStruct((bricks * 2, 4, TILE), f32),
        in_specs=[smem, smem, vmem],
        out_specs=vmem,
        scratch_shapes=[
            pltpu.SMEM((bricks,), jnp.int32),
            pltpu.VMEM((4, TILE, TILE), f32),
            pltpu.VMEM((4, TILE, TILE), f32),
        ],
        compiler_params=pltpu.CompilerParams(vmem_limit_bytes=16 << 20),
        name="pack",
    )(dest, block, pos)


def splat(arrived, nx, ny, nz):
    _, vmem, _ = specs()
    records = arrived.shape[0]
    strip = jax.ShapeDtypeStruct((HALO, ny, nz), f32)
    return pl.pallas_call(
        splat_kernel,
        out_shape=(jax.ShapeDtypeStruct((nx, ny, nz), f32), strip, strip),
        in_specs=[vmem],
        out_specs=(vmem, vmem, vmem),
        scratch_shapes=[
            pltpu.SMEM((8, 128), jnp.int32),
            pltpu.SemaphoreType.DMA,
            pltpu.VMEM((8, 128), jnp.int32),
            pltpu.VMEM((records, 128), f32),
            pltpu.VMEM((3 * TILE, 3 * records), jnp.bfloat16),
            pltpu.VMEM((TILE * records // 8, 128), f32),
            pltpu.VMEM((TILE * records // 8, 128), f32),
            pltpu.VMEM((TILE * records // 8, 128), f32),
            pltpu.VMEM((TILE * BLOCK, 8, 128), f32),
            pltpu.VMEM((BLOCK * BLOCK * 8, 128), f32),
            pltpu.VMEM((2, nx, ny, 128), f32),
        ],
        compiler_params=pltpu.CompilerParams(vmem_limit_bytes=40 << 20),
        name="splat",
    )(arrived)


def jacobi(level, kind, divergence, level_halo, input_halo):
    _, vmem, hbm = specs()
    nx, ny, nz = divergence.shape
    ext = (nx + 2 * HALO, 2, ny + 2 * ROWS, 128)
    lxl, lxh, lyl, lyh = level_halo
    ixl, ixh, iyl, iyh = input_halo
    return pl.pallas_call(
        jacobi_kernel,
        out_shape=jax.ShapeDtypeStruct((nx, ny, nz), f32),
        in_specs=[hbm] * 7 + [vmem] * 4,
        out_specs=vmem,
        scratch_shapes=[pltpu.VMEM(ext, f32)] * 6 + [pltpu.SemaphoreType.DMA((3, 3, 2))],
        compiler_params=pltpu.CompilerParams(vmem_limit_bytes=48 << 20),
        name="jacobi",
    )(level, kind, divergence, lxl, lxh, ixl, ixh, lyl, lyh, iyl, iyh)


def shifts(axis):
    count = lax.axis_size(axis)
    forward = [(i, i + 1) for i in range(count - 1)]
    return forward, [(j, i) for i, j in forward]


def swap(axis, low_part, high_part):
    forward, backward = shifts(axis)
    return lax.ppermute(high_part, axis, forward), lax.ppermute(low_part, axis, backward)


def halo_y(block, xl, xh):
    H = HALO
    low = jnp.concatenate([xl[..., :H, :], block[..., :H, :], xh[..., :H, :]], axis=-3)
    high = jnp.concatenate([xl[..., -H:, :], block[..., -H:, :], xh[..., -H:, :]], axis=-3)
    return swap("gy", low, high)


def per_device(particle_pos, tile_dest, tile_block, fluid_flag, divergence):
    nx, ny, nz = divergence.shape
    bricks = lax.axis_size("gx") * lax.axis_size("gy")

    kind = 5.0 - 4.0 * fluid_flag.astype(f32)
    both = jnp.stack([kind, divergence])
    ixl, ixh = swap("gx", both[:, :HALO], both[:, -HALO:])
    iyl, iyh = halo_y(both, ixl, ixh)

    send = pack(tile_dest[:, 0], tile_block, particle_pos, bricks)
    arrived = lax.all_to_all(send, ("gx", "gy"), split_axis=0, concat_axis=0, tiled=True)
    level, low, high = splat(arrived, nx, ny, nz)
    lxl, lxh = swap("gx", low, high)
    lyl, lyh = halo_y(level, lxl, lxh)
    pressure = jacobi(level, kind, divergence, (lxl, lxh, lyl, lyh), (ixl, ixh, iyl, iyh))
    return (level, pressure)


def solution(mesh):
    placed = (
        P(None, ("gx", "gy")),
        P(("gx", "gy"), None),
        P(("gx", "gy")),
        P("gx", "gy", None),
        P("gx", "gy", None),
    )
    return jax.shard_map(
        per_device,
        mesh=mesh,
        in_specs=placed,
        out_specs=(P("gx", "gy", None), P("gx", "gy", None)),
        check_vma=False,
    )
```

time: 197 us -> 139 us (0.71)
  the two profiles are of different devices: /device:TPU:13 before, /device:TPU:20 now
where the time goes in v2:
time: 139 us; the launch traced here: 136 us
  starting transfers between devices  66.8 us (48%)
  Pallas kernels  54 us (39%)
  other arithmetic  5.03 us (4%)
  waiting for transfers between devices  4.71 us (3%)
  local copies, waits for them, and re-layouts  4.6 us (3%)
    ppermute x4, starting transfers between devices, swap(): lax.ppermute(high_part, axis, forward)  36.5 us
    pallas_call x1, Pallas kernels, splat(): pl.pallas_call(splat_kernel, out_shape=(jax.ShapeDtypeStruct((nx, ny, nz)...  35.2 us
    ppermute x4, starting transfers between devices, swap(): lax.ppermute(low_part, axis, backward)  20 us
    pallas_call x1, Pallas kernels, jacobi(): pl.pallas_call(jacobi_kernel, out_shape=jax.ShapeDtypeStruct((nx, ny, nz)...  14.7 us
    all_to_all x1, starting transfers between devices, per_device(): lax.all_to_all(send, ('gx', 'gy'), split_axis=0, concat_axis=0, tiled=True)  10.3 us
    pallas_call x1, Pallas kernels, pack(): pl.pallas_call(pack_kernel, out_shape=jax.ShapeDtypeStruct((bricks * 2, 4...  4.16 us
    ppermute x4, waiting for transfers between devices, swap(): lax.ppermute(high_part, axis, forward)  3.88 us
    unnamed x12, local copies, waits for them, and re-layouts  3.48 us
  transfers between devices with their start and end apart: 9, of which 2 were waited for; matrix products, arithmetic and copies ran while one was open for 5% of the time, Pallas kernels for 26%

profile of v2, /device:TPU:20, one launch (start us, length us, event | category | flops | bytes accessed | tf_op | source)
XLA Modules:
  0.0 136.0 jit_solution(8578174131199506377)
XLA Ops:
  0.6 0.0 copy-start.1
  0.6 0.9 copy-done.1
  1.6 0.0 copy-start.2
  1.6 0.7 copy-done.2
  2.2 0.0 copy-start.3
  2.2 0.7 copy-done.3
  2.9 4.2 %pack.1 = f32[256,4,128]{2,1,0:T(4,128)} custom-call(s32[128]{0:T(128)S(1)} %bitcast.4, s32[128]{0:T(128)S(1)} %copy-done.3, f32[3,16384]{1,0:T(4,128)S(1)} %copy-done.1), custom_call_target="tpu_custom_call" | custom-call | tf_op jit(solution)/shard_map/pack/pallas_call | solution.py:412
  7.1 10.3 %all-to-all-start = ((f32[256,4,128]{2,1,0:T(4,128)}), f32[256,4,128]{2,1,0:T(4,128)S(1)}, u32[]{:S(2)}, u32[]{:S(2)}) async-start(f32[256,4,128]{2,1,0:T(4,128)} %pack.1), calls=%async_computation | async-start | bytes 1048576 | tf_op jit(solution)/shard_map/all_to_all | solution.py:499
  17.4 0.0 copy-start.5
  17.4 3.4 %fusion.4 = (f32[1,32,64,256]{3,2,1,0:T(8,128)S(1)}, f32[32,64,256]{2,1,0:T(8,128)}) fusion(s32[32,64,256]{2,1,0:T(8,128)} %param.8), kind=kLoop, calls=%fused_computation.11 | loop fusion | flops 1572864 | bytes 6291456 | tf_op jit(solution)/shard_map/stack | solution.py:494
  20.8 0.0 copy-start.4
  20.8 0.0 copy-done.5
  20.8 0.1 pad_maximum_fusion
  20.9 1.2 copy-done.4
  22.1 3.6 %collective-permute-start.2 = (f32[2,4,64,256]{3,2,1,0:T(8,128)S(1)}, f32[2,4,64,256]{3,2,1,0:T(8,128)S(1)}, u32[]{:S(2)}, u32[]{:S(2)}) collective-permute-start(f32[2,4,64,256]{3,2,1,0:T(8,128)S(1)} %get-tuple-element.11), channel_id=1, source_target_pairs={{0,8},{8,16},{16,24},{24,32},{32,40},{40,48},{48,56},{56,64},{64,7... | collective-permute-start | bytes 1572872 | tf_op jit(solution)/shard_map/ppermute | solution.py:479
  25.7 4.3 %collective-permute-start.3 = (f32[2,4,64,256]{3,2,1,0:T(8,128)S(1)}, f32[2,4,64,256]{3,2,1,0:T(8,128)S(1)}, u32[]{:S(2)}, u32[]{:S(2)}) collective-permute-start(f32[2,4,64,256]{3,2,1,0:T(8,128)S(1)} %get-tuple-element.10), channel_id=1, source_target_pairs={{8,0},{16,8},{24,16},{32,24},{40,32},{48,40},{56,48},{64,56},{72,6... | collective-permute-start | bytes 1572872 | tf_op jit(solution)/shard_map/ppermute | solution.py:479
  30.0 0.0 all-to-all-done.rec_ref
  30.0 35.2 %splat.1 = (f32[32,64,256]{2,1,0:T(8,128)}, f32[4,64,256]{2,1,0:T(8,128)S(1)}, f32[4,64,256]{2,1,0:T(8,128)S(1)}) custom-call(f32[256,4,128]{2,1,0:T(4,128)S(1)} %all-to-all-done.rec_ref), custom_call_target="tpu_custom_call" | custom-call | tf_op jit(solution)/shard_map/splat/pallas_call | solution.py:431
  65.2 1.9 %collective-permute-start = (f32[4,64,256]{2,1,0:T(8,128)S(1)}, f32[4,64,256]{2,1,0:T(8,128)S(1)}, u32[]{:S(2)}, u32[]{:S(2)}) collective-permute-start(f32[4,64,256]{2,1,0:T(8,128)S(1)} %get-tuple-element.6), channel_id=1, source_target_pairs={{0,8},{8,16},{16,24},{24,32},{32,40},{40,48},{48,56},{56,64},{64,7... | collective-permute-start | bytes 786440 | tf_op jit(solution)/shard_map/ppermute | solution.py:479
  67.1 6.0 %collective-permute-start.1 = (f32[4,64,256]{2,1,0:T(8,128)S(1)}, f32[4,64,256]{2,1,0:T(8,128)S(1)}, u32[]{:S(2)}, u32[]{:S(2)}) collective-permute-start(f32[4,64,256]{2,1,0:T(8,128)S(1)} %get-tuple-element.7), channel_id=1, source_target_pairs={{8,0},{16,8},{24,16},{32,24},{40,32},{48,40},{56,48},{64,56},{72,6... | collective-permute-start | bytes 786440 | tf_op jit(solution)/shard_map/ppermute | solution.py:479
  73.2 1.1 fusion.5
  74.3 0.0 collective-permute-done.2.ixl_ref
  74.3 0.0 collective-permute-done.3.ixh_ref
  74.3 0.0 copy-start
  74.3 1.5 %fusion.1 = (f32[2,40,4,256]{3,2,1,0:T(4,128)S(1)}, f32[2,40,4,256]{3,2,1,0:T(4,128)S(1)}) fusion(f32[1,32,64,256]{3,2,1,0:T(8,128)} %bitcast.5, f32[1,32,64,256]{3,2,1,0:T(8,128)} %copy-done.4, f32[2,4,4,256]{3,2,1,0:T(4,128)S(1)} %get-tuple-element.18, f32[2,4,4,256]{3,2,1,0:T(4,128)S(1)} %get-tuple-element.16, f32[2,4,4,256]{3,2,1,0:T(4,128)S(1)} %get-tuple-element.19, ...), kind=kLoop, calls=%fused_computation.5 | loop fusion | flops 491520 | bytes 4980736 | tf_op jit(solution)/shard_map/concatenate | solution.py:484
  75.8 29.0 %collective-permute-start.6 = (f32[2,40,4,256]{3,2,1,0:T(4,128)S(1)}, f32[2,40,4,256]{3,2,1,0:T(4,128)S(1)}, u32[]{:S(2)}, u32[]{:S(2)}) collective-permute-start(f32[2,40,4,256]{3,2,1,0:T(4,128)S(1)} %get-tuple-element.9), channel_id=1, source_target_pairs={{0,1},{1,2},{2,3},{3,4},{4,5},{5,6},{6,7},{8,9},{9,10},{10,11},{11... | collective-permute-start | bytes 983048 | tf_op jit(solution)/shard_map/ppermute | solution.py:479
  104.8 1.9 %collective-permute-start.7 = (f32[2,40,4,256]{3,2,1,0:T(4,128)S(1)}, f32[2,40,4,256]{3,2,1,0:T(4,128)S(1)}, u32[]{:S(2)}, u32[]{:S(2)}) collective-permute-start(f32[2,40,4,256]{3,2,1,0:T(4,128)S(1)} %get-tuple-element.8), channel_id=1, source_target_pairs={{1,0},{2,1},{3,2},{4,3},{5,4},{6,5},{7,6},{9,8},{10,9},{11,10},{12... | collective-permute-start | bytes 983048 | tf_op jit(solution)/shard_map/ppermute | solution.py:479
  106.8 0.0 collective-permute-done.lxl_ref
  106.8 0.0 collective-permute-done.1.lxh_ref
  106.9 7.8 %collective-permute-start.5 = (f32[40,4,256]{2,1,0:T(4,128)S(1)}, f32[40,4,256]{2,1,0:T(4,128)S(1)}, u32[]{:S(2)}, u32[]{:S(2)}) collective-permute-start(f32[40,4,256]{2,1,0:T(4,128)S(1)} %pad_maximum_fusion.5), channel_id=1, source_target_pairs={{1,0},{2,1},{3,2},{4,3},{5,4},{6,5},{7,6},{9,8},{10,9},{11,10},{12... | collective-permute-start | bytes 491528 | tf_op jit(solution)/shard_map/ppermute | solution.py:479
  114.7 1.9 %collective-permute-start.4 = (f32[40,4,256]{2,1,0:T(4,128)S(1)}, f32[40,4,256]{2,1,0:T(4,128)S(1)}, u32[]{:S(2)}, u32[]{:S(2)}) collective-permute-start(f32[40,4,256]{2,1,0:T(4,128)S(1)} %pad_maximum_fusion.4), channel_id=1, source_target_pairs={{0,1},{1,2},{2,3},{3,4},{4,5},{5,6},{6,7},{8,9},{9,10},{10,11},{11... | collective-permute-start | bytes 491528 | tf_op jit(solution)/shard_map/ppermute | solution.py:479
  116.6 0.0 collective-permute-done.6.iyl_ref
  116.6 0.0 collective-permute-done.7.iyh_ref
  116.6 0.8 collective-permute-done.5.lyh_ref
  117.4 3.9 %collective-permute-done.4.lyl_ref = f32[40,4,256]{2,1,0:T(4,128)S(1)} collective-permute-done((f32[40,4,256]{2,1,0:T(4,128)S(1)}, f32[40,4,256]{2,1,0:T(4,128)S(1)}, u32[]{:S(2)}, u32[]{:S(2)}) %collective-permute-start.4) | collective-permute-done | bytes 163872 | tf_op jit(solution)/shard_map/ppermute | solution.py:479
  121.3 0.0 copy-done
  121.3 14.7 %jacobi.1 = f32[32,64,256]{2,1,0:T(8,128)} custom-call(f32[32,64,256]{2,1,0:T(8,128)S(1)} %copy-done, f32[32,64,256]{2,1,0:T(8,128)} %get-tuple-element.15.kind_ref, f32[32,64,256]{2,1,0:T(8,128)} %div_ref.1, f32[4,64,256]{2,1,0:T(8,128)S(1)} %collective-permute-done.lxl_ref, f32[4,64,256]{2,1,0:T(8,128)S(1)} %collective-permute-done.1.lxh_ref, ...), custom_call_target="tpu_custom_call" | custom-call | tf_op jit(solution)/shard_map/jacobi/pallas_call | solution.py:460
  (6 shorter events, 0.1 us)
Async XLA Ops:
  0.6 1.0 copy-start.1
  1.6 0.7 copy-start.2
  2.2 0.7 copy-start.3
  7.1 23.0 %all-to-all-start = ((f32[256,4,128]{2,1,0:T(4,128)}), f32[256,4,128]{2,1,0:T(4,128)S(1)}, u32[]{:S(2)}, u32[]{:S(2)}) async-start(f32[256,4,128]{2,1,0:T(4,128)} %pack.1), calls=%async_computation | async-start | bytes 1048576 | tf_op jit(solution)/shard_map/all_to_all | solution.py:499
  17.4 3.4 %copy-start.5 = (f32[32,64,256]{2,1,0:T(8,128)S(1)}, f32[32,64,256]{2,1,0:T(8,128)}, u32[]{:S(2)}) copy-start(f32[32,64,256]{2,1,0:T(8,128)} %div_ref.1) | copy-start | bytes 6291460
  20.8 1.3 copy-start.4
  22.1 52.2 %collective-permute-start.2 = (f32[2,4,64,256]{3,2,1,0:T(8,128)S(1)}, f32[2,4,64,256]{3,2,1,0:T(8,128)S(1)}, u32[]{:S(2)}, u32[]{:S(2)}) collective-permute-start(f32[2,4,64,256]{3,2,1,0:T(8,128)S(1)} %get-tuple-element.11), channel_id=1, source_target_pairs={{0,8},{8,16},{16,24},{24,32},{32,40},{40,48},{48,56},{56,64},{64,7... | collective-permute-start | bytes 1572872 | tf_op jit(solution)/shard_map/ppermute | solution.py:479
  25.7 48.6 %collective-permute-start.3 = (f32[2,4,64,256]{3,2,1,0:T(8,128)S(1)}, f32[2,4,64,256]{3,2,1,0:T(8,128)S(1)}, u32[]{:S(2)}, u32[]{:S(2)}) collective-permute-start(f32[2,4,64,256]{3,2,1,0:T(8,128)S(1)} %get-tuple-element.10), channel_id=1, source_target_pairs={{8,0},{16,8},{24,16},{32,24},{40,32},{48,40},{56,48},{64,56},{72,6... | collective-permute-start | bytes 1572872 | tf_op jit(solution)/shard_map/ppermute | solution.py:479
  65.2 41.5 %collective-permute-start = (f32[4,64,256]{2,1,0:T(8,128)S(1)}, f32[4,64,256]{2,1,0:T(8,128)S(1)}, u32[]{:S(2)}, u32[]{:S(2)}) collective-permute-start(f32[4,64,256]{2,1,0:T(8,128)S(1)} %get-tuple-element.6), channel_id=1, source_target_pairs={{0,8},{8,16},{16,24},{24,32},{32,40},{40,48},{48,56},{56,64},{64,7... | collective-permute-start | bytes 786440 | tf_op jit(solution)/shard_map/ppermute | solution.py:479
  67.1 39.6 %collective-permute-start.1 = (f32[4,64,256]{2,1,0:T(8,128)S(1)}, f32[4,64,256]{2,1,0:T(8,128)S(1)}, u32[]{:S(2)}, u32[]{:S(2)}) collective-permute-start(f32[4,64,256]{2,1,0:T(8,128)S(1)} %get-tuple-element.7), channel_id=1, source_target_pairs={{8,0},{16,8},{24,16},{32,24},{40,32},{48,40},{56,48},{64,56},{72,6... | collective-permute-start | bytes 786440 | tf_op jit(solution)/shard_map/ppermute | solution.py:479
  74.3 47.0 %copy-start = (f32[32,64,256]{2,1,0:T(8,128)S(1)}, f32[32,64,256]{2,1,0:T(8,128)}, u32[]{:S(2)}) copy-start(f32[32,64,256]{2,1,0:T(8,128)} %get-tuple-element.3.level_ref) | copy-start | bytes 6291460
  75.8 40.8 %collective-permute-start.6 = (f32[2,40,4,256]{3,2,1,0:T(4,128)S(1)}, f32[2,40,4,256]{3,2,1,0:T(4,128)S(1)}, u32[]{:S(2)}, u32[]{:S(2)}) collective-permute-start(f32[2,40,4,256]{3,2,1,0:T(4,128)S(1)} %get-tuple-element.9), channel_id=1, source_target_pairs={{0,1},{1,2},{2,3},{3,4},{4,5},{5,6},{6,7},{8,9},{9,10},{10,11},{11... | collective-permute-start | bytes 983048 | tf_op jit(solution)/shard_map/ppermute | solution.py:479
  104.8 11.8 %collective-permute-start.7 = (f32[2,40,4,256]{3,2,1,0:T(4,128)S(1)}, f32[2,40,4,256]{3,2,1,0:T(4,128)S(1)}, u32[]{:S(2)}, u32[]{:S(2)}) collective-permute-start(f32[2,40,4,256]{3,2,1,0:T(4,128)S(1)} %get-tuple-element.8), channel_id=1, source_target_pairs={{1,0},{2,1},{3,2},{4,3},{5,4},{6,5},{7,6},{9,8},{10,9},{11,10},{12... | collective-permute-start | bytes 983048 | tf_op jit(solution)/shard_map/ppermute | solution.py:479
  106.9 10.6 %collective-permute-start.5 = (f32[40,4,256]{2,1,0:T(4,128)S(1)}, f32[40,4,256]{2,1,0:T(4,128)S(1)}, u32[]{:S(2)}, u32[]{:S(2)}) collective-permute-start(f32[40,4,256]{2,1,0:T(4,128)S(1)} %pad_maximum_fusion.5), channel_id=1, source_target_pairs={{1,0},{2,1},{3,2},{4,3},{5,4},{6,5},{7,6},{9,8},{10,9},{11,10},{12... | collective-permute-start | bytes 491528 | tf_op jit(solution)/shard_map/ppermute | solution.py:479
  114.7 6.6 %collective-permute-start.4 = (f32[40,4,256]{2,1,0:T(4,128)S(1)}, f32[40,4,256]{2,1,0:T(4,128)S(1)}, u32[]{:S(2)}, u32[]{:S(2)}) collective-permute-start(f32[40,4,256]{2,1,0:T(4,128)S(1)} %pad_maximum_fusion.4), channel_id=1, source_target_pairs={{0,1},{1,2},{2,3},{3,4},{4,5},{5,6},{6,7},{8,9},{9,10},{10,11},{11... | collective-permute-start | bytes 491528 | tf_op jit(solution)/shard_map/ppermute | solution.py:479

commit v3 on v2

--- a/solution.py
+++ b/solution.py
@@ -69,8 +69,14 @@
     return data
 
 
-def pack_kernel(dest_ref, block_ref, pos_ref, send_ref, count_ref, tile_ref, turn_ref):
+def pack_kernel(dest_in, block_in, pos_in, send_ref, dest_ref, block_ref, pos_ref, count_ref, tile_ref, turn_ref, sem):
     tiles = block_ref.shape[0]
+    copies = [
+        pltpu.make_async_copy(a, b, sem.at[n])
+        for n, (a, b) in enumerate(((pos_in, pos_ref), (dest_in, dest_ref), (block_in, block_ref)))
+    ]
+    for copy in copies:
+        copy.start()
     lane = lax.broadcasted_iota(jnp.int32, (4, TILE), 1)
     note = (lax.broadcasted_iota(jnp.int32, (4, TILE), 0) == 3) & (lane == 0)
 
@@ -79,9 +85,10 @@
         return carry
 
     lax.fori_loop(0, count_ref.shape[0], clear, 0)
-    empty = jnp.where(lane == 0, -1.0, jnp.where(lane <= PAIRS, float(TILE), 0.0)).astype(f32)
+    empty = jnp.where(lane == 0, -1.0, 0.0).astype(f32)
     send_ref[...] = jnp.broadcast_to(empty[None], send_ref.shape)
 
+    copies[0].wait()
     for t in range(tiles):
         tile_ref[0:3, t, :] = pos_ref[:, t * TILE : t * TILE + TILE]
     parts = []
@@ -96,7 +103,7 @@
         for v in range(16):
             below = below + jnp.where(parts[0][v] < 2 * k + 0.5 - REACH, 1.0, 0.0)
             upto = upto + jnp.where(parts[0][v] < 2 * k + 1.5 + REACH, 1.0, 0.0)
-        turn_ref[3, 1 + k : 2 + k, :] = jnp.sum(below, axis=0, keepdims=True)
+        turn_ref[3, 1 + k : 2 + k, :] = jnp.sum(below, axis=0, keepdims=True) - TILE
         turn_ref[3, 1 + PAIRS + k : 2 + PAIRS + k, :] = -jnp.sum(upto, axis=0, keepdims=True)
     for c in range(3):
         for v in range(16):
@@ -104,6 +111,9 @@
     for c in range(4):
         tile_ref[c] = jnp.transpose(turn_ref[c], (1, 0))
 
+    copies[1].wait()
+    copies[2].wait()
+
     def place(t, carry):
         owner = dest_ref[t]
         slot = count_ref[owner]
@@ -118,19 +128,33 @@
     return jnp.where(condition, 1.0, 0.0).astype(jnp.bfloat16)
 
 
+def row_to_column(row):
+    return jnp.concatenate(
+        [
+            jnp.transpose(jnp.broadcast_to(row[:, h : h + 128], (128, 128)), (1, 0))
+            for h in range(0, row.shape[1], 128)
+        ],
+        axis=0,
+    )
+
+
 def arrange(notes, note_ref, slot_ref):
     records = notes.shape[0]
     halves = records // 128
-    turned = [jnp.transpose(notes[h * 128 : h * 128 + 128, :], (1, 0))[0:1, :] for h in range(halves)]
-    labels = jnp.concatenate(turned, axis=1)
+    turned = [jnp.transpose(notes[h * 128 : h * 128 + 128, :], (1, 0)) for h in range(halves)]
+    labels = jnp.concatenate([v[0:1, :] for v in turned], axis=1)
+    keys = jnp.concatenate([jnp.sum(v[1 : 1 + 2 * PAIRS], axis=0, keepdims=True) for v in turned], axis=1)
     valid = labels >= 0.0
     spot = (labels.astype(jnp.int32) & 7).astype(f32)
     column = lax.broadcasted_iota(jnp.int32, (8, records), 0).astype(f32)
     member = jnp.where(valid & (column == spot), 1.0, 0.0)
-    earlier = ones_where(
-        lax.broadcasted_iota(jnp.int32, (records, records), 0) < lax.broadcasted_iota(jnp.int32, (records, records), 1)
-    )
-    before = jnp.dot(member.astype(jnp.bfloat16), earlier, preferred_element_type=f32)
+    from_index = lax.broadcasted_iota(jnp.int32, (records, records), 0)
+    to_index = lax.broadcasted_iota(jnp.int32, (records, records), 1)
+    earlier = ones_where(from_index < to_index)
+    own = row_to_column(keys)
+    own = jnp.concatenate([own] * halves, axis=1)
+    smaller = (own < keys) | ((own == keys) & (from_index < to_index))
+    before = jnp.dot(member.astype(jnp.bfloat16), ones_where(smaller), preferred_element_type=f32)
     rank = jnp.sum(member * before, axis=0, keepdims=True)
     counts = jnp.sum(member, axis=1, keepdims=True)
     total = jnp.sum(counts, axis=0, keepdims=True)
@@ -146,66 +170,73 @@
     chosen = (turn >= offset) & (turn < offset + free)
     moved = jnp.sum(jnp.where(chosen, (used + turn - offset) * 8.0 + column, 0.0), axis=0, keepdims=True)
     slots = jnp.where(valid, jnp.where(late > 0.0, moved, rank * 8.0 + spot), -1.0)
-    for h in range(halves):
-        part = jnp.broadcast_to(slots[:, h * 128 : h * 128 + 128], (128, 128))
-        slot_ref[h * 128 : h * 128 + 128, :] = jnp.transpose(part, (1, 0))
+    slot_ref[...] = slots
     lane = lax.broadcasted_iota(jnp.int32, (records, 128), 1).astype(f32)
     raised = jnp.broadcast_to(jnp.where(valid, labels + 1.0, 0.0), (8, records)).astype(jnp.bfloat16)
+    late_slots = jnp.broadcast_to(jnp.where(late > 0.0, slots + 1.0, 0.0), (8, records)).astype(jnp.bfloat16)
+    to_slot = row_to_column(slots)
+    to_turn = row_to_column(jnp.where(late > 0.0, turn, -1.0))
     for h in range(halves):
-        here = jnp.dot(raised, ones_where(slot_ref[...] == lane + 128.0 * h), preferred_element_type=f32)
+        here = jnp.dot(raised, ones_where(to_slot == lane + 128.0 * h), preferred_element_type=f32)
         note_ref[h : h + 1, :] = (here[0:1] - 1.0).astype(jnp.int32)
-    least = jnp.min(notes, axis=0, keepdims=True)
-    note_ref[halves : halves + 1, :] = jnp.where(lane[0:1] == 0.0, total, least).astype(jnp.int32)
-
-
-def splat_kernel(rec_ref, out_ref, low_ref, high_ref, meta_ref, sem,
-                 note_ref, slot_ref, split_ref, px_ref, py_ref, pz_ref, dyz_ref, acc_ref, near_ref):
+        here = jnp.dot(late_slots, ones_where(to_turn == lane + 128.0 * h), preferred_element_type=f32)
+        note_ref[halves + h : halves + h + 1, :] = here[0:1].astype(jnp.int32)
+    sums = jnp.where(lane[0:1] == 0.0, total, jnp.sum(late, axis=1, keepdims=True))
+    note_ref[2 * halves : 2 * halves + 1, :] = sums.astype(jnp.int32)
+
+
+def splat_kernel(spread_ref, rec_ref, out_ref, low_ref, high_ref, meta_ref, sem,
+                 note_ref, slot_ref, piece_ref, turn_ref, px_ref, py_ref, pz_ref, dyz_ref, acc_ref, near_ref):
     records = rec_ref.shape[0]
     halves = records // 128
-    groups = records // 8
-    nx = out_ref.shape[0]
-
-    arrange(rec_ref[:, 3, :], note_ref, slot_ref)
+    nx, ny = out_ref.shape[0:2]
+
+    notes = rec_ref[:, 3, :]
+    arrange(notes, note_ref, slot_ref)
+    index = lax.broadcasted_iota(jnp.int32, (records, records), 0).astype(f32)
+    to_slot = ones_where(index == slot_ref[...])
+    pieces = [[], [], []]
+    for c in range(3):
+        whole = rec_ref[:, c, :]
+        high = whole.astype(jnp.bfloat16)
+        rest = whole - high.astype(f32)
+        middle = rest.astype(jnp.bfloat16)
+        pieces[0].append(high)
+        pieces[1].append(middle)
+        pieces[2].append((rest - middle.astype(f32)).astype(jnp.bfloat16))
+    for n in range(3):
+        for c in range(3):
+            piece_ref[n * 3 + c] = jnp.dot(to_slot, pieces[n][c], preferred_element_type=f32)
+    placed = jnp.dot(to_slot, notes.astype(jnp.bfloat16), preferred_element_type=f32)
+    for b in range(records // 64):
+        least = jnp.min(placed[b * 64 : b * 64 + 64, :], axis=0, keepdims=True)
+        note_ref[2 * halves + 1 + b : 2 * halves + 2 + b, :] = least.astype(jnp.int32)
     copy = pltpu.make_async_copy(note_ref, meta_ref, sem)
     copy.start()
     near_ref[...] = jnp.full(near_ref.shape, FAR, f32)
-    for c in range(3):
-        for h in range(halves):
-            whole = jnp.transpose(rec_ref[h * 128 : h * 128 + 128, c, :], (1, 0))
-            high = whole.astype(jnp.bfloat16)
-            rest = whole - high.astype(f32)
-            middle = rest.astype(jnp.bfloat16)
-            last = (rest - middle.astype(f32)).astype(jnp.bfloat16)
-            for n, part in enumerate((high, middle, last)):
-                at = n * records + h * 128
-                split_ref[c * TILE : c * TILE + TILE, at : at + 128] = part
+    turn_ref[...] = jnp.zeros(turn_ref.shape, f32)
     copy.wait()
-    batches = (meta_ref[halves, 0] + 63) // 64
+    batches = (meta_ref[2 * halves, 0] + 63) // 64
+    late = meta_ref[2 * halves, 1]
 
     lane = lax.broadcasted_iota(jnp.int32, (8, 128), 1)
     depth = (lane & 15).astype(f32) + 0.5
     spots = lax.broadcasted_iota(jnp.int32, (1, 128), 1) >> 4
-    tile_lane = (lax.broadcasted_iota(jnp.int32, (records, 128), 1) >> 4).astype(f32)
-
-    def expand(q, carry):
-        slot = slot_ref[...] - (q * 16).astype(f32)
-        hit = jnp.concatenate([ones_where(slot == tile_lane), ones_where(slot == tile_lane + 8.0)], axis=1)
-        place = jnp.dot(split_ref[...], jnp.concatenate([hit] * 3, axis=0), preferred_element_type=f32)
-        for n in range(2):
-            rows = pl.ds(q * 2 + n, TILE, stride=groups)
-            lanes = slice(n * 128, n * 128 + 128)
-            px_ref[rows, :] = place[0:TILE, lanes]
-            py_ref[rows, :] = place[TILE : 2 * TILE, lanes]
-            pz_ref[rows, :] = place[2 * TILE : 3 * TILE, lanes]
-        return carry
-
-    lax.fori_loop(0, batches * 4, expand, 0)
 
     def batch(g, carry):
+        for s in range(8):
+            for n in range(9):
+                turn_ref[s, n * 8 : n * 8 + 8, :] = piece_ref[n, pl.ds(pl.multiple_of(g * 64 + s * 8, 8), 8), :]
+            turned = jnp.transpose(turn_ref[s], (1, 0)).astype(jnp.bfloat16)
+            place = jnp.dot(turned, spread_ref[...], preferred_element_type=f32)
+            px_ref[pl.ds(s, TILE, stride=8), :] = place[:, 0:128]
+            py_ref[pl.ds(s, TILE, stride=8), :] = place[:, 128:256]
+            pz_ref[pl.ds(s, TILE, stride=8), :] = place[:, 256:384]
+
         def prepare(k, inner):
-            for u in range(2):
-                p = k * 2 + u
-                rows = pl.ds(pl.multiple_of(p * groups + g * 8, 8), 8)
+            for u in range(8):
+                p = k * 8 + u
+                rows = pl.ds(pl.multiple_of(p * 8, 8), 8)
                 py = py_ref[rows, :]
                 dz = depth - pz_ref[rows, :]
                 dz = dz * dz
@@ -214,11 +245,11 @@
                     dyz_ref[p * 16 + y] = dy * dy + dz
             return inner
 
-        lax.fori_loop(0, TILE // 2, prepare, 0)
+        lax.fori_loop(0, TILE // 8, prepare, 0)
 
         for k in range(PAIRS):
-            stop = -meta_ref[halves, 1 + PAIRS + k]
-            steps = (stop - meta_ref[halves, 1 + k] + 7) // 8
+            stop = -meta_ref[2 * halves + 1 + g, 1 + PAIRS + k]
+            steps = (stop - (meta_ref[2 * halves + 1 + g, 1 + k] + TILE) + 7) // 8
             first = jnp.maximum(stop - steps * 8, 0)
 
             def step(i, accs):
@@ -227,7 +258,7 @@
                     p = first + i * 8 + u * 2
                     away = []
                     for v in range(2):
-                        px = px_ref[pl.ds(pl.multiple_of((p + v) * groups + g * 8, 8), 8), :]
+                        px = px_ref[pl.ds(pl.multiple_of((p + v) * 8, 8), 8), :]
                         d0 = (2 * k + 0.5) - px
                         d1 = (2 * k + 1.5) - px
                         away.append((d0 * d0, d1 * d1))
@@ -243,49 +274,45 @@
             for i in range(32):
                 acc_ref[(k * 32 + i) * 8 : (k * 32 + i) * 8 + 8, :] = accs[i]
 
-        def put_down(s, t, move):
-            label = meta_ref[g // 2, g % 2 * 64 + s * 8 + t]
-            spot = label & 7
-            wanted = (label >= 0) & ((spot == t) != move)
-            mask = spots == jnp.where(wanted, spot, -1)
-            label = jnp.maximum(label, 0)
+        def put_down(s, t, label, mask, move):
             bx = label // 64
-            ys = pl.ds(pl.multiple_of(label // 16 % 4 * 16, 16), 16)
-            half = label // 8 % 2
-
-            def update():
-                for x in range(16):
-                    tile = acc_ref[pl.ds(x * 128 + s, 16, stride=8), :]
-                    if move:
-                        tile = pltpu.roll(tile, ((spot - t) & 7) * 16, 1)
-                    tile = jnp.where(mask, tile, FAR)
-                    near_ref[half, bx * 16 + x, ys, :] = jnp.minimum(near_ref[half, bx * 16 + x, ys, :], tile)
-
-            if move:
-                pl.when(wanted)(update)
-            else:
-                update()
+            base = (label // 8 % 2) * (nx * ny) + bx * (16 * ny) + label // 16 % 4 * 16
+            for x in range(16):
+                tile = acc_ref[pl.ds(x * 128 + s, 16, stride=8), :]
+                if move is not None:
+                    tile = pltpu.roll(tile, move, 1)
+                rows = pl.ds(pl.multiple_of(base + x * ny, 16), 16)
+                near_ref[rows, :] = jnp.minimum(near_ref[rows, :], jnp.where(mask, tile, FAR))
 
         def merge(t, inner):
             for s in range(8):
-                put_down(s, t, False)
+                label = meta_ref[g // 2, g % 2 * 64 + s * 8 + t]
+                wanted = (label >= 0) & ((label & 7) == t)
+                put_down(s, t, jnp.maximum(label, 0), spots == jnp.where(wanted, t, -1), None)
             return inner
 
         lax.fori_loop(0, 8, merge, 0)
 
-        def merge_late(t, inner):
-            for s in range(8):
-                put_down(s, t, True)
+        def merge_late(i, inner):
+            j = meta_ref[halves + i // 128, i % 128] - 1
+
+            @pl.when(j // 64 == g)
+            def _():
+                t = j % 8
+                label = meta_ref[j // 128, j % 128]
+                spot = label & 7
+                put_down(j // 8 % 8, t, label, spots == spot, ((spot - t) & 7) * 16)
+
             return inner
 
-        lax.fori_loop(0, 8, merge_late, 0)
+        lax.fori_loop(0, late, merge_late, 0)
         return carry
 
     lax.fori_loop(0, batches, batch, 0)
 
     def finish(x, carry):
         for half in range(2):
-            out_ref[x, :, half * 128 : half * 128 + 128] = jnp.minimum(jnp.sqrt(near_ref[half, x]) - RADIUS, BAND)
+            out_ref[x, :, half * 128 : half * 128 + 128] = jnp.minimum(jnp.sqrt(near_ref[pl.ds(pl.multiple_of(half * nx * ny + x * ny, ny), ny), :]) - RADIUS, BAND)
         return carry
 
     lax.fori_loop(0, nx, finish, 0)
@@ -404,20 +431,24 @@
 
 
 def specs():
-    return pl.BlockSpec(memory_space=pltpu.SMEM), pl.BlockSpec(memory_space=pltpu.VMEM), pl.BlockSpec(memory_space=pl.ANY)
+    return tuple(pl.BlockSpec(memory_space=space) for space in (pltpu.VMEM, pl.ANY, pltpu.HBM))
 
 
 def pack(dest, block, pos, bricks):
-    smem, vmem, _ = specs()
+    vmem, _, hbm = specs()
     return pl.pallas_call(
         pack_kernel,
         out_shape=jax.ShapeDtypeStruct((bricks * 2, 4, TILE), f32),
-        in_specs=[smem, smem, vmem],
+        in_specs=[hbm] * 3,
         out_specs=vmem,
         scratch_shapes=[
+            pltpu.SMEM(dest.shape, jnp.int32),
+            pltpu.SMEM(block.shape, jnp.int32),
+            pltpu.VMEM(pos.shape, f32),
             pltpu.SMEM((bricks,), jnp.int32),
             pltpu.VMEM((4, TILE, TILE), f32),
             pltpu.VMEM((4, TILE, TILE), f32),
+            pltpu.SemaphoreType.DMA((3,)),
         ],
         compiler_params=pltpu.CompilerParams(vmem_limit_bytes=16 << 20),
         name="pack",
@@ -425,34 +456,35 @@
 
 
 def splat(arrived, nx, ny, nz):
-    _, vmem, _ = specs()
+    vmem, _, _ = specs()
     records = arrived.shape[0]
     strip = jax.ShapeDtypeStruct((HALO, ny, nz), f32)
     return pl.pallas_call(
         splat_kernel,
         out_shape=(jax.ShapeDtypeStruct((nx, ny, nz), f32), strip, strip),
-        in_specs=[vmem],
+        in_specs=[vmem, vmem],
         out_specs=(vmem, vmem, vmem),
         scratch_shapes=[
-            pltpu.SMEM((8, 128), jnp.int32),
+            pltpu.SMEM((16, 128), jnp.int32),
             pltpu.SemaphoreType.DMA,
-            pltpu.VMEM((8, 128), jnp.int32),
-            pltpu.VMEM((records, 128), f32),
-            pltpu.VMEM((3 * TILE, 3 * records), jnp.bfloat16),
-            pltpu.VMEM((TILE * records // 8, 128), f32),
-            pltpu.VMEM((TILE * records // 8, 128), f32),
-            pltpu.VMEM((TILE * records // 8, 128), f32),
+            pltpu.VMEM((16, 128), jnp.int32),
+            pltpu.VMEM((1, records), f32),
+            pltpu.VMEM((9, records, TILE), f32),
+            pltpu.VMEM((8, 128, TILE), f32),
+            pltpu.VMEM((TILE * 8, 128), f32),
+            pltpu.VMEM((TILE * 8, 128), f32),
+            pltpu.VMEM((TILE * 8, 128), f32),
             pltpu.VMEM((TILE * BLOCK, 8, 128), f32),
             pltpu.VMEM((BLOCK * BLOCK * 8, 128), f32),
-            pltpu.VMEM((2, nx, ny, 128), f32),
+            pltpu.VMEM((2 * nx * ny, 128), f32),
         ],
         compiler_params=pltpu.CompilerParams(vmem_limit_bytes=40 << 20),
         name="splat",
-    )(arrived)
+    )(spread_matrix(), arrived)
 
 
 def jacobi(level, kind, divergence, level_halo, input_halo):
-    _, vmem, hbm = specs()
+    vmem, hbm, _ = specs()
     nx, ny, nz = divergence.shape
     ext = (nx + 2 * HALO, 2, ny + 2 * ROWS, 128)
     lxl, lxh, lyl, lyh = level_halo
@@ -468,6 +500,15 @@
     )(level, kind, divergence, lxl, lxh, ixl, ixh, lyl, lyh, iyl, iyh)
 
 
+def spread_matrix():
+    row = jnp.arange(128)
+    coord, tile = row // 8 % 3, row % 8
+    column = jnp.arange(384)
+    hit = (row[:, None] < 72) & (coord[:, None] == column[None, :] // 128)
+    hit = hit & (tile[:, None] == column[None, :] % 128 // 16)
+    return hit.astype(jnp.bfloat16)
+
+
 def shifts(axis):
     count = lax.axis_size(axis)
     forward = [(i, i + 1) for i in range(count - 1)]
@@ -491,12 +532,14 @@
     bricks = lax.axis_size("gx") * lax.axis_size("gy")
 
     kind = 5.0 - 4.0 * fluid_flag.astype(f32)
-    both = jnp.stack([kind, divergence])
-    ixl, ixh = swap("gx", both[:, :HALO], both[:, -HALO:])
-    iyl, iyh = halo_y(both, ixl, ixh)
+    pair = (kind, divergence)
+    ixl, ixh = swap("gx", jnp.stack([v[:HALO] for v in pair]), jnp.stack([v[-HALO:] for v in pair]))
+    edge = jnp.stack([jnp.concatenate([v[:, :HALO], v[:, -HALO:]], axis=1) for v in pair])
+    iyl, iyh = halo_y(edge, ixl, ixh)
 
     send = pack(tile_dest[:, 0], tile_block, particle_pos, bricks)
     arrived = lax.all_to_all(send, ("gx", "gy"), split_axis=0, concat_axis=0, tiled=True)
+    arrived, iyl, iyh = lax.optimization_barrier((arrived, iyl, iyh))
     level, low, high = splat(arrived, nx, ny, nz)
     lxl, lxh = swap("gx", low, high)
     lyl, lyh = halo_y(level, lxl, lxh)

time: 139 us -> 150 us (1.079)
  the two profiles are of different devices: /device:TPU:20 before, /device:TPU:3 now
where the time goes in v3:
time: 150 us; the launch traced here: 149 us
  starting transfers between devices  64 us (43%)
  Pallas kernels  47.3 us (32%)
  waiting for transfers between devices  26.8 us (18%)
  local copies, waits for them, and re-layouts  7.59 us (5%)
  other arithmetic  2.46 us (2%)
    ppermute x4, starting transfers between devices, swap(): lax.ppermute(high_part, axis, forward)  38.9 us
    pallas_call x1, Pallas kernels, splat(): pl.pallas_call(splat_kernel, out_shape=(jax.ShapeDtypeStruct((nx, ny, nz)...  28.8 us
    ppermute x4, waiting for transfers between devices, swap(): lax.ppermute(low_part, axis, backward)  18.7 us
    pallas_call x1, Pallas kernels, jacobi(): pl.pallas_call(jacobi_kernel, out_shape=jax.ShapeDtypeStruct((nx, ny, nz)...  14.7 us
    ppermute x4, starting transfers between devices, swap(): lax.ppermute(low_part, axis, backward)  14.3 us
    all_to_all x1, starting transfers between devices, per_device(): lax.all_to_all(send, ('gx', 'gy'), split_axis=0, concat_axis=0, tiled=True)  10.8 us
    ppermute x4, waiting for transfers between devices, swap(): lax.ppermute(high_part, axis, forward)  8.01 us
    unnamed x10, local copies, waits for them, and re-layouts  3.85 us
  transfers between devices with their start and end apart: 9, of which 8 were waited for; matrix products, arithmetic and copies ran while one was open for 4% of the time, Pallas kernels for 0%

profile of v3, /device:TPU:3, one launch (start us, length us, event | category | flops | bytes accessed | tf_op | source)
XLA Modules:
  0.0 149.0 jit_solution(4690975467704586139)
XLA Ops:
  0.6 0.0 copy-start.1
  0.6 0.9 copy-done.1
  1.6 0.0 copy-start.2
  1.6 0.7 copy-done.2
  2.2 0.0 copy-start.3
  2.2 0.7 copy-done.3
  2.9 3.8 %pack.1 = f32[256,4,128]{2,1,0:T(4,128)} custom-call(s32[128]{0:T(128)S(1)} %bitcast.13, s32[128]{0:T(128)S(1)} %copy-done.3, f32[3,16384]{1,0:T(4,128)S(1)} %copy-done.1), custom_call_target="tpu_custom_call" | custom-call | tf_op jit(solution)/shard_map/pack/pallas_call | solution.py:439
  6.7 10.8 %all-to-all-start = ((f32[256,4,128]{2,1,0:T(4,128)}), f32[256,4,128]{2,1,0:T(4,128)S(1)}, u32[]{:S(2)}, u32[]{:S(2)}) async-start(f32[256,4,128]{2,1,0:T(4,128)} %pack.1), calls=%async_computation | async-start | bytes 1048576 | tf_op jit(solution)/shard_map/all_to_all | solution.py:541
  17.6 1.9 %multiply_subtract_fusion.kind_ref = f32[32,64,256]{2,1,0:T(8,128)S(1)} fusion(s32[32,64,256]{2,1,0:T(8,128)} %param.8), kind=kLoop, calls=%fused_computation | loop fusion | flops 1572864 | bytes 4194304 | tf_op jit(solution)/shard_map/sub | solution.py:534
  19.5 0.0 copy-start.4
  19.5 1.5 slice_bitcast_fusion.1
  21.0 5.0 %collective-permute-start.1 = (f32[2,4,64,256]{3,2,1,0:T(8,128)S(1)}, f32[2,4,64,256]{3,2,1,0:T(8,128)S(1)}, u32[]{:S(2)}, u32[]{:S(2)}) collective-permute-start(f32[2,4,64,256]{3,2,1,0:T(8,128)S(1)} %pad_maximum_fusion.1), channel_id=1, source_target_pairs={{8,0},{16,8},{24,16},{32,24},{40,32},{48,40},{56,48},{64,56},{72,6... | collective-permute-start | bytes 1572872 | tf_op jit(solution)/shard_map/ppermute | solution.py:520
  26.0 1.9 %collective-permute-start = (f32[2,4,64,256]{3,2,1,0:T(8,128)S(1)}, f32[2,4,64,256]{3,2,1,0:T(8,128)S(1)}, u32[]{:S(2)}, u32[]{:S(2)}) collective-permute-start(f32[2,4,64,256]{3,2,1,0:T(8,128)S(1)} %pad_maximum_fusion), channel_id=1, source_target_pairs={{0,8},{8,16},{16,24},{24,32},{32,40},{40,48},{48,56},{56,64},{64,7... | collective-permute-start | bytes 1572872 | tf_op jit(solution)/shard_map/ppermute | solution.py:520
  27.9 1.1 fusion.14
  29.0 0.0 copy-done.4
  29.1 0.1 maximum_bitcast_fusion
  29.2 0.1 fusion.2
  29.3 8.4 %collective-permute-done.1.ixh_ref = f32[2,4,64,256]{3,2,1,0:T(8,128)S(1)} collective-permute-done((f32[2,4,64,256]{3,2,1,0:T(8,128)S(1)}, f32[2,4,64,256]{3,2,1,0:T(8,128)S(1)}, u32[]{:S(2)}, u32[]{:S(2)}) %collective-permute-start.1) | collective-permute-done | bytes 524320 | tf_op jit(solution)/shard_map/ppermute | solution.py:520
  37.7 5.2 %collective-permute-done.ixl_ref = f32[2,4,64,256]{3,2,1,0:T(8,128)S(1)} collective-permute-done((f32[2,4,64,256]{3,2,1,0:T(8,128)S(1)}, f32[2,4,64,256]{3,2,1,0:T(8,128)S(1)}, u32[]{:S(2)}, u32[]{:S(2)}) %collective-permute-start) | collective-permute-done | bytes 524320 | tf_op jit(solution)/shard_map/ppermute | solution.py:520
  42.9 0.1 pad_maximum_fusion.3
  43.0 4.6 %collective-permute-start.2 = (f32[2,40,4,256]{3,2,1,0:T(4,128)S(1)}, f32[2,40,4,256]{3,2,1,0:T(4,128)S(1)}, u32[]{:S(2)}, u32[]{:S(2)}) collective-permute-start(f32[2,40,4,256]{3,2,1,0:T(4,128)S(1)} %pad_maximum_fusion.3), channel_id=1, source_target_pairs={{0,1},{1,2},{2,3},{3,4},{4,5},{5,6},{6,7},{8,9},{9,10},{10,11},{11... | collective-permute-start | bytes 983048 | tf_op jit(solution)/shard_map/ppermute | solution.py:520
  47.5 0.1 fusion.1
  47.6 1.9 %collective-permute-start.3 = (f32[2,40,4,256]{3,2,1,0:T(4,128)S(1)}, f32[2,40,4,256]{3,2,1,0:T(4,128)S(1)}, u32[]{:S(2)}, u32[]{:S(2)}) collective-permute-start(f32[2,40,4,256]{3,2,1,0:T(4,128)S(1)} %fusion.1), channel_id=1, source_target_pairs={{1,0},{2,1},{3,2},{4,3},{5,4},{6,5},{7,6},{9,8},{10,9},{11,10},{12... | collective-permute-start | bytes 983048 | tf_op jit(solution)/shard_map/ppermute | solution.py:520
  49.5 0.1 and_convert_fusion.spread_ref
  49.6 0.0 all-to-all-done.rec_ref
  49.7 1.9 %collective-permute-done.2.iyl_ref = f32[2,40,4,256]{3,2,1,0:T(4,128)S(1)} collective-permute-done((f32[2,40,4,256]{3,2,1,0:T(4,128)S(1)}, f32[2,40,4,256]{3,2,1,0:T(4,128)S(1)}, u32[]{:S(2)}, u32[]{:S(2)}) %collective-permute-start.2) | collective-permute-done | bytes 327712 | tf_op jit(solution)/shard_map/ppermute | solution.py:520
  51.5 4.5 %collective-permute-done.3.iyh_ref = f32[2,40,4,256]{3,2,1,0:T(4,128)S(1)} collective-permute-done((f32[2,40,4,256]{3,2,1,0:T(4,128)S(1)}, f32[2,40,4,256]{3,2,1,0:T(4,128)S(1)}, u32[]{:S(2)}, u32[]{:S(2)}) %collective-permute-start.3) | collective-permute-done | bytes 327712 | tf_op jit(solution)/shard_map/ppermute | solution.py:520
  56.0 28.8 %splat.1 = (f32[32,64,256]{2,1,0:T(8,128)}, f32[4,64,256]{2,1,0:T(8,128)S(1)}, f32[4,64,256]{2,1,0:T(8,128)S(1)}) custom-call(bf16[128,384]{1,0:T(8,128)(2,1)S(1)} %and_convert_fusion.spread_ref, f32[256,4,128]{2,1,0:T(4,128)S(1)} %all-to-all-done.rec_ref), custom_call_target="tpu_custom_call" | custom-call | tf_op jit(solution)/shard_map/splat/pallas_call | solution.py:462
  84.8 1.9 %collective-permute-start.4 = (f32[4,64,256]{2,1,0:T(8,128)S(1)}, f32[4,64,256]{2,1,0:T(8,128)S(1)}, u32[]{:S(2)}, u32[]{:S(2)}) collective-permute-start(f32[4,64,256]{2,1,0:T(8,128)S(1)} %get-tuple-element.10), channel_id=1, source_target_pairs={{0,8},{8,16},{16,24},{24,32},{32,40},{40,48},{48,56},{56,64},{64,7... | collective-permute-start | bytes 786440 | tf_op jit(solution)/shard_map/ppermute | solution.py:520
  86.7 5.5 %collective-permute-start.5 = (f32[4,64,256]{2,1,0:T(8,128)S(1)}, f32[4,64,256]{2,1,0:T(8,128)S(1)}, u32[]{:S(2)}, u32[]{:S(2)}) collective-permute-start(f32[4,64,256]{2,1,0:T(8,128)S(1)} %get-tuple-element.11), channel_id=1, source_target_pairs={{8,0},{16,8},{24,16},{32,24},{40,32},{48,40},{56,48},{64,56},{72,6... | collective-permute-start | bytes 786440 | tf_op jit(solution)/shard_map/ppermute | solution.py:520
  92.2 1.1 fusion.13
  93.3 0.7 collective-permute-done.4.lxl_ref
  94.0 1.5 collective-permute-done.5.lxh_ref
  95.5 30.5 %collective-permute-start.6 = (f32[40,4,256]{2,1,0:T(4,128)S(1)}, f32[40,4,256]{2,1,0:T(4,128)S(1)}, u32[]{:S(2)}, u32[]{:S(2)}) collective-permute-start(f32[40,4,256]{2,1,0:T(4,128)S(1)} %pad_maximum_fusion.4), channel_id=1, source_target_pairs={{0,1},{1,2},{2,3},{3,4},{4,5},{5,6},{6,7},{8,9},{9,10},{10,11},{11... | collective-permute-start | bytes 491528 | tf_op jit(solution)/shard_map/ppermute | solution.py:520
  126.1 1.9 %collective-permute-start.7 = (f32[40,4,256]{2,1,0:T(4,128)S(1)}, f32[40,4,256]{2,1,0:T(4,128)S(1)}, u32[]{:S(2)}, u32[]{:S(2)}) collective-permute-start(f32[40,4,256]{2,1,0:T(4,128)S(1)} %pad_maximum_fusion.5), channel_id=1, source_target_pairs={{1,0},{2,1},{3,2},{4,3},{5,4},{6,5},{7,6},{9,8},{10,9},{11,10},{12... | collective-permute-start | bytes 491528 | tf_op jit(solution)/shard_map/ppermute | solution.py:520
  128.1 0.3 collective-permute-done.6.lyl_ref
  128.3 4.4 %collective-permute-done.7.lyh_ref = f32[40,4,256]{2,1,0:T(4,128)S(1)} collective-permute-done((f32[40,4,256]{2,1,0:T(4,128)S(1)}, f32[40,4,256]{2,1,0:T(4,128)S(1)}, u32[]{:S(2)}, u32[]{:S(2)}) %collective-permute-start.7) | collective-permute-done | bytes 163872 | tf_op jit(solution)/shard_map/ppermute | solution.py:520
  132.8 0.0 copy-start
  132.8 1.6 %copy-done = f32[32,64,256]{2,1,0:T(8,128)S(1)} copy-done((f32[32,64,256]{2,1,0:T(8,128)S(1)}, f32[32,64,256]{2,1,0:T(8,128)}, u32[]{:S(2)}) %copy-start) | copy-done | bytes 2097176
  134.4 14.7 %jacobi.1 = f32[32,64,256]{2,1,0:T(8,128)} custom-call(f32[32,64,256]{2,1,0:T(8,128)S(1)} %copy-done, f32[32,64,256]{2,1,0:T(8,128)} %copy-done.4, f32[32,64,256]{2,1,0:T(8,128)} %div_ref.1, f32[4,64,256]{2,1,0:T(8,128)S(1)} %collective-permute-done.4.lxl_ref, f32[4,64,256]{2,1,0:T(8,128)S(1)} %collective-permute-done.5.lxh_ref, ...), custom_call_target="tpu_custom_call" | custom-call | tf_op jit(solution)/shard_map/jacobi/pallas_call | solution.py:492
  (12 shorter events, 0.3 us)
Async XLA Ops:
  0.6 1.0 copy-start.1
  1.6 0.7 copy-start.2
  2.2 0.7 copy-start.3
  6.7 42.9 %all-to-all-start = ((f32[256,4,128]{2,1,0:T(4,128)}), f32[256,4,128]{2,1,0:T(4,128)S(1)}, u32[]{:S(2)}, u32[]{:S(2)}) async-start(f32[256,4,128]{2,1,0:T(4,128)} %pack.1), calls=%async_computation | async-start | bytes 1048576 | tf_op jit(solution)/shard_map/all_to_all | solution.py:541
  19.5 9.6 %copy-start.4 = (f32[32,64,256]{2,1,0:T(8,128)}, f32[32,64,256]{2,1,0:T(8,128)S(1)}, u32[]{:S(2)}) copy-start(f32[32,64,256]{2,1,0:T(8,128)S(1)} %multiply_subtract_fusion.kind_ref) | copy-start | bytes 6291460
  21.0 16.7 %collective-permute-start.1 = (f32[2,4,64,256]{3,2,1,0:T(8,128)S(1)}, f32[2,4,64,256]{3,2,1,0:T(8,128)S(1)}, u32[]{:S(2)}, u32[]{:S(2)}) collective-permute-start(f32[2,4,64,256]{3,2,1,0:T(8,128)S(1)} %pad_maximum_fusion.1), channel_id=1, source_target_pairs={{8,0},{16,8},{24,16},{32,24},{40,32},{48,40},{56,48},{64,56},{72,6... | collective-permute-start | bytes 1572872 | tf_op jit(solution)/shard_map/ppermute | solution.py:520
  26.0 16.8 %collective-permute-start = (f32[2,4,64,256]{3,2,1,0:T(8,128)S(1)}, f32[2,4,64,256]{3,2,1,0:T(8,128)S(1)}, u32[]{:S(2)}, u32[]{:S(2)}) collective-permute-start(f32[2,4,64,256]{3,2,1,0:T(8,128)S(1)} %pad_maximum_fusion), channel_id=1, source_target_pairs={{0,8},{8,16},{16,24},{24,32},{32,40},{40,48},{48,56},{56,64},{64,7... | collective-permute-start | bytes 1572872 | tf_op jit(solution)/shard_map/ppermute | solution.py:520
  43.0 8.6 %collective-permute-start.2 = (f32[2,40,4,256]{3,2,1,0:T(4,128)S(1)}, f32[2,40,4,256]{3,2,1,0:T(4,128)S(1)}, u32[]{:S(2)}, u32[]{:S(2)}) collective-permute-start(f32[2,40,4,256]{3,2,1,0:T(4,128)S(1)} %pad_maximum_fusion.3), channel_id=1, source_target_pairs={{0,1},{1,2},{2,3},{3,4},{4,5},{5,6},{6,7},{8,9},{9,10},{10,11},{11... | collective-permute-start | bytes 983048 | tf_op jit(solution)/shard_map/ppermute | solution.py:520
  47.6 8.4 %collective-permute-start.3 = (f32[2,40,4,256]{3,2,1,0:T(4,128)S(1)}, f32[2,40,4,256]{3,2,1,0:T(4,128)S(1)}, u32[]{:S(2)}, u32[]{:S(2)}) collective-permute-start(f32[2,40,4,256]{3,2,1,0:T(4,128)S(1)} %fusion.1), channel_id=1, source_target_pairs={{1,0},{2,1},{3,2},{4,3},{5,4},{6,5},{7,6},{9,8},{10,9},{11,10},{12... | collective-permute-start | bytes 983048 | tf_op jit(solution)/shard_map/ppermute | solution.py:520
  84.8 9.2 %collective-permute-start.4 = (f32[4,64,256]{2,1,0:T(8,128)S(1)}, f32[4,64,256]{2,1,0:T(8,128)S(1)}, u32[]{:S(2)}, u32[]{:S(2)}) collective-permute-start(f32[4,64,256]{2,1,0:T(8,128)S(1)} %get-tuple-element.10), channel_id=1, source_target_pairs={{0,8},{8,16},{16,24},{24,32},{32,40},{40,48},{48,56},{56,64},{64,7... | collective-permute-start | bytes 786440 | tf_op jit(solution)/shard_map/ppermute | solution.py:520
  86.7 8.8 %collective-permute-start.5 = (f32[4,64,256]{2,1,0:T(8,128)S(1)}, f32[4,64,256]{2,1,0:T(8,128)S(1)}, u32[]{:S(2)}, u32[]{:S(2)}) collective-permute-start(f32[4,64,256]{2,1,0:T(8,128)S(1)} %get-tuple-element.11), channel_id=1, source_target_pairs={{8,0},{16,8},{24,16},{32,24},{40,32},{48,40},{56,48},{64,56},{72,6... | collective-permute-start | bytes 786440 | tf_op jit(solution)/shard_map/ppermute | solution.py:520
  95.5 32.8 %collective-permute-start.6 = (f32[40,4,256]{2,1,0:T(4,128)S(1)}, f32[40,4,256]{2,1,0:T(4,128)S(1)}, u32[]{:S(2)}, u32[]{:S(2)}) collective-permute-start(f32[40,4,256]{2,1,0:T(4,128)S(1)} %pad_maximum_fusion.4), channel_id=1, source_target_pairs={{0,1},{1,2},{2,3},{3,4},{4,5},{5,6},{6,7},{8,9},{9,10},{10,11},{11... | collective-permute-start | bytes 491528 | tf_op jit(solution)/shard_map/ppermute | solution.py:520
  126.1 6.6 %collective-permute-start.7 = (f32[40,4,256]{2,1,0:T(4,128)S(1)}, f32[40,4,256]{2,1,0:T(4,128)S(1)}, u32[]{:S(2)}, u32[]{:S(2)}) collective-permute-start(f32[40,4,256]{2,1,0:T(4,128)S(1)} %pad_maximum_fusion.5), channel_id=1, source_target_pairs={{1,0},{2,1},{3,2},{4,3},{5,4},{6,5},{7,6},{9,8},{10,9},{11,10},{12... | collective-permute-start | bytes 491528 | tf_op jit(solution)/shard_map/ppermute | solution.py:520
  132.8 1.6 %copy-start = (f32[32,64,256]{2,1,0:T(8,128)S(1)}, f32[32,64,256]{2,1,0:T(8,128)}, u32[]{:S(2)}) copy-start(f32[32,64,256]{2,1,0:T(8,128)} %get-tuple-element.6.level_ref) | copy-start | bytes 6291460

commit v4 on v3

--- a/solution.py
+++ b/solution.py
@@ -143,7 +143,8 @@
     halves = records // 128
     turned = [jnp.transpose(notes[h * 128 : h * 128 + 128, :], (1, 0)) for h in range(halves)]
     labels = jnp.concatenate([v[0:1, :] for v in turned], axis=1)
-    keys = jnp.concatenate([jnp.sum(v[1 : 1 + 2 * PAIRS], axis=0, keepdims=True) for v in turned], axis=1)
+    shift = [v[1 : 1 + PAIRS] - v[1 + PAIRS : 1 + 2 * PAIRS] for v in turned]
+    keys = jnp.concatenate([jnp.sum(v, axis=0, keepdims=True) for v in shift], axis=1)
     valid = labels >= 0.0
     spot = (labels.astype(jnp.int32) & 7).astype(f32)
     column = lax.broadcasted_iota(jnp.int32, (8, records), 0).astype(f32)
@@ -182,10 +183,65 @@
         here = jnp.dot(late_slots, ones_where(to_turn == lane + 128.0 * h), preferred_element_type=f32)
         note_ref[halves + h : halves + h + 1, :] = here[0:1].astype(jnp.int32)
     sums = jnp.where(lane[0:1] == 0.0, total, jnp.sum(late, axis=1, keepdims=True))
+    for b in range(records // 64):
+        here = jnp.where((slots >= 64.0 * b) & (slots < 64.0 * b + 64.0), late, 0.0)
+        sums = jnp.where(lane[0:1] == 2.0 + b, jnp.sum(here, axis=1, keepdims=True), sums)
     note_ref[2 * halves : 2 * halves + 1, :] = sums.astype(jnp.int32)
 
 
-def splat_kernel(spread_ref, rec_ref, out_ref, low_ref, high_ref, meta_ref, sem,
+def strips_kernel(side_ref, kind_in, div_in, first_ref, second_ref, face1_ref, face2_ref, kx_ref, ky_ref, dy_ref, sem):
+    nx, ny, nz = kind_in.shape
+    copies = []
+    side = side_ref[0]
+    for n, (at, out) in enumerate((((1 - side) * (nx - HALO), first_ref), (side * (nx - HALO), second_ref))):
+        planes = pl.ds(at, HALO)
+        copies.append(pltpu.make_async_copy(kind_in.at[planes], kx_ref.at[n], sem.at[n]))
+        copies.append(pltpu.make_async_copy(div_in.at[planes], out.at[1], sem.at[2 + n]))
+    for n, at in enumerate((0, ny - 8)):
+        rows = pl.ds(at, 8)
+        copies.append(pltpu.make_async_copy(kind_in.at[:, rows, :], ky_ref.at[n], sem.at[4 + n]))
+        copies.append(pltpu.make_async_copy(div_in.at[:, rows, :], dy_ref.at[n], sem.at[6 + n]))
+    for copy in copies:
+        copy.start()
+    for copy in copies:
+        copy.wait()
+    first_ref[0] = kind_of(kx_ref[0])
+    second_ref[0] = kind_of(kx_ref[1])
+    low = slice(0, HALO)
+    high = slice(8 - HALO, 8)
+    even = side_ref[1] == 0
+    for turn, out in ((True, face1_ref), (False, face2_ref)):
+        up = even if turn else jnp.logical_not(even)
+        out[0] = jnp.where(up, kind_of(ky_ref[1, :, high, :]), kind_of(ky_ref[0, :, low, :]))
+        out[1] = jnp.where(up, dy_ref[1, :, high, :], dy_ref[0, :, low, :])
+
+
+def strips(side, flag, divergence):
+    vmem, hbm, _ = specs()
+    nx, ny, nz = divergence.shape
+    strip = jax.ShapeDtypeStruct((2, HALO, ny, nz), f32)
+    edge = jax.ShapeDtypeStruct((2, nx, HALO, nz), f32)
+    return pl.pallas_call(
+        strips_kernel,
+        out_shape=(strip, strip, edge, edge),
+        in_specs=[scalars(), hbm, hbm],
+        out_specs=(vmem,) * 4,
+        scratch_shapes=[
+            pltpu.VMEM((2, HALO, ny, nz), jnp.int32),
+            pltpu.VMEM((2, nx, 8, nz), jnp.int32),
+            pltpu.VMEM((2, nx, 8, nz), f32),
+            pltpu.SemaphoreType.DMA((8,)),
+        ],
+        compiler_params=pltpu.CompilerParams(vmem_limit_bytes=60 << 20),
+        name="strips",
+    )(side, flag, divergence)
+
+
+def kind_of(flag):
+    return 5.0 - 4.0 * flag.astype(f32)
+
+
+def splat_kernel(side_ref, spread_ref, rec_ref, out_ref, halves_ref, first_ref, second_ref, left_ref, right_ref, meta_ref, sem,
                  note_ref, slot_ref, piece_ref, turn_ref, px_ref, py_ref, pz_ref, dyz_ref, acc_ref, near_ref):
     records = rec_ref.shape[0]
     halves = records // 128
@@ -305,50 +361,78 @@
 
             return inner
 
-        lax.fori_loop(0, late, merge_late, 0)
+        lax.fori_loop(0, jnp.where(meta_ref[2 * halves, 2 + g] > 0, late, 0), merge_late, 0)
         return carry
 
     lax.fori_loop(0, batches, batch, 0)
 
     def finish(x, carry):
         for half in range(2):
-            out_ref[x, :, half * 128 : half * 128 + 128] = jnp.minimum(jnp.sqrt(near_ref[pl.ds(pl.multiple_of(half * nx * ny + x * ny, ny), ny), :]) - RADIUS, BAND)
+            lanes = slice(half * 128, half * 128 + 128)
+            rows = pl.ds(pl.multiple_of(half * nx * ny + x * ny, ny), ny)
+            level = jnp.minimum(jnp.sqrt(near_ref[rows, :]) - RADIUS, BAND)
+            out_ref[x, :, lanes] = level
+            size = jnp.abs(level)
+            halves_ref[x, half] = size
+            left_ref[x, :, lanes] = size[0:HALO, :]
+            right_ref[x, :, lanes] = size[ny - HALO : ny, :]
         return carry
 
     lax.fori_loop(0, nx, finish, 0)
-    low_ref[...] = out_ref[0:HALO]
-    high_ref[...] = out_ref[nx - HALO : nx]
-
-
-def jacobi_kernel(level_ref, kind_ref, div_ref, lxl_ref, lxh_ref, ixl_ref, ixh_ref, lyl_ref, lyh_ref, iyl_ref, iyh_ref, out_ref,
-                  a_ref, u_ref, d_ref, c_ref, p_ref, q_ref, sem):
+    side = side_ref[0]
+    first_ref[...] = jnp.abs(out_ref[pl.ds((1 - side) * (nx - HALO), HALO)])
+    second_ref[...] = jnp.abs(out_ref[pl.ds(side * (nx - HALO), HALO)])
+
+
+def jacobi_kernel(side_ref, level_ref, flag_ref, div_ref, lx1_ref, lx2_ref, ix1_ref, ix2_ref, ly1_ref, ly2_ref, iy1_ref, iy2_ref, out_ref,
+                  a_ref, u_ref, d_ref, c_ref, p_ref, q_ref, f_ref, sem):
     nx, ny, nz = out_ref.shape
     H = HALO
     R = ROWS
     copies = []
-    for n, (mid, low, high, ext) in enumerate(
-        (
-            (kind_ref, ixl_ref.at[0], ixh_ref.at[0], u_ref),
-            (div_ref, ixl_ref.at[1], ixh_ref.at[1], d_ref),
-            (level_ref, lxl_ref, lxh_ref, a_ref),
-        )
-    ):
-        for half in range(2):
-            lanes = pl.ds(half * 128, 128)
-            for m, (source, at, size) in enumerate(((mid, H, nx), (low, 0, H), (high, nx + H, H))):
-                copies.append(
-                    pltpu.make_async_copy(
-                        source.at[:, :, lanes], ext.at[pl.ds(at, size), half, pl.ds(R, ny), :], sem.at[n, m, half]
-                    )
-                )
+    inner = pl.ds(R, ny)
+    side = side_ref[0]
+    mid_x = pl.ds(H, nx)
+    first_x, second_x = pl.ds((1 - side) * (nx + H), H), pl.ds(side * (nx + H), H)
+    for half in range(2):
+        lanes = pl.ds(half * 128, 128)
+        for n, (source, target) in enumerate(
+            (
+                (flag_ref, f_ref.at[:, half]),
+                (ix1_ref.at[0], u_ref.at[first_x, half, inner]),
+                (ix2_ref.at[0], u_ref.at[second_x, half, inner]),
+                (div_ref, d_ref.at[mid_x, half, inner]),
+                (ix1_ref.at[1], d_ref.at[first_x, half, inner]),
+                (ix2_ref.at[1], d_ref.at[second_x, half, inner]),
+                (lx1_ref, a_ref.at[first_x, half, inner]),
+                (lx2_ref, a_ref.at[second_x, half, inner]),
+            )
+        ):
+            copies.append(pltpu.make_async_copy(source.at[:, :, lanes], target, sem.at[n, half]))
+    copies.append(pltpu.make_async_copy(level_ref, a_ref.at[mid_x, :, inner], sem.at[8, 0]))
     for copy in copies:
         copy.start()
-    for low, high, ext in ((lyl_ref, lyh_ref, a_ref), (iyl_ref.at[0], iyh_ref.at[0], u_ref), (iyl_ref.at[1], iyh_ref.at[1], d_ref)):
-        for half in range(2):
-            lanes = slice(half * 128, half * 128 + 128)
-            ext[:, half, R - H : R, :] = low[:, :, lanes]
-            ext[:, half, R + ny : R + ny + H, :] = high[:, :, lanes]
-    for copy in copies:
+    for half in range(2):
+        lanes = slice(half * 128, half * 128 + 128)
+        for turn, rows in ((1, slice(R - H, R)), (0, slice(R + ny, R + ny + H))):
+            first = side_ref[1] == turn
+            a_ref[:, half, rows, :] = jnp.where(first, ly1_ref[0 : nx + 2 * H, :, lanes], ly2_ref[0 : nx + 2 * H, :, lanes])
+            for n, ext in enumerate((u_ref, d_ref)):
+                at = nx + 2 * H + n * 2 * H
+                corner = jnp.where(first, ly1_ref[at : at + 2 * H, :, lanes], ly2_ref[at : at + 2 * H, :, lanes])
+                ext[0:H, half, rows, :] = corner[0:H]
+                ext[nx + H : nx + 2 * H, half, rows, :] = corner[H : 2 * H]
+                ext[H : nx + H, half, rows, :] = jnp.where(first, iy1_ref[n, :, :, lanes], iy2_ref[n, :, :, lanes])
+    copies[0].wait()
+    copies[8].wait()
+
+    def convert(x, carry):
+        for h in range(2):
+            u_ref[x + H, h, R : R + ny, :] = kind_of(f_ref[x, h])
+        return carry
+
+    lax.fori_loop(0, nx, convert, 0, unroll=2)
+    for copy in copies[1:8] + copies[9:]:
         copy.wait()
 
     lane = lax.broadcasted_iota(jnp.int32, (8, 128), 1)
@@ -366,7 +450,7 @@
     def coefficient(x, carry):
         r0, rows = R - H, ny + 2 * H
         at = slice(r0, r0 + rows)
-        mags = [jnp.abs(a_ref[x, h, at, :]) for h in range(2)]
+        mags = [a_ref[x, h, at, :] for h in range(2)]
         kinds = [u_ref[x, h, at, :] for h in range(2)]
         za, zu = along(mags, rows), along(kinds, rows)
         for h in range(2):
@@ -376,7 +460,7 @@
             near = [(za[h][0], zu[h][0]), (za[h][1], zu[h][1])]
             for dx, dy in ((-1, 0), (1, 0), (0, -1), (0, 1)):
                 beside = slice(r0 + dy, r0 + dy + rows)
-                near.append((jnp.abs(a_ref[x + dx, h, beside, :]), u_ref[x + dx, h, beside, :]))
+                near.append((a_ref[x + dx, h, beside, :], u_ref[x + dx, h, beside, :]))
             for b, w in near:
                 term = jnp.minimum(jnp.maximum(a + b, 1.0) * r, w)
                 diagonal = term if diagonal is None else diagonal + term
@@ -432,6 +516,10 @@
 
 def specs():
     return tuple(pl.BlockSpec(memory_space=space) for space in (pltpu.VMEM, pl.ANY, pltpu.HBM))
+
+
+def scalars():
+    return pl.BlockSpec(memory_space=pltpu.SMEM)
 
 
 def pack(dest, block, pos, bricks):
@@ -450,20 +538,28 @@
             pltpu.VMEM((4, TILE, TILE), f32),
             pltpu.SemaphoreType.DMA((3,)),
         ],
-        compiler_params=pltpu.CompilerParams(vmem_limit_bytes=16 << 20),
+        compiler_params=pltpu.CompilerParams(vmem_limit_bytes=60 << 20),
         name="pack",
     )(dest, block, pos)
 
 
-def splat(arrived, nx, ny, nz):
+def splat(side, arrived, nx, ny, nz):
     vmem, _, _ = specs()
     records = arrived.shape[0]
     strip = jax.ShapeDtypeStruct((HALO, ny, nz), f32)
+    edge = jax.ShapeDtypeStruct((nx, HALO, nz), f32)
     return pl.pallas_call(
         splat_kernel,
-        out_shape=(jax.ShapeDtypeStruct((nx, ny, nz), f32), strip, strip),
-        in_specs=[vmem, vmem],
-        out_specs=(vmem, vmem, vmem),
+        out_shape=(
+            jax.ShapeDtypeStruct((nx, ny, nz), f32),
+            jax.ShapeDtypeStruct((nx, 2, ny, 128), f32),
+            strip,
+            strip,
+            edge,
+            edge,
+        ),
+        in_specs=[scalars(), vmem, vmem],
+        out_specs=(vmem,) * 6,
         scratch_shapes=[
             pltpu.SMEM((16, 128), jnp.int32),
             pltpu.SemaphoreType.DMA,
@@ -480,24 +576,57 @@
         ],
         compiler_params=pltpu.CompilerParams(vmem_limit_bytes=40 << 20),
         name="splat",
-    )(spread_matrix(), arrived)
-
-
-def jacobi(level, kind, divergence, level_halo, input_halo):
+    )(side, spread_matrix(), arrived)
+
+
+def edges_kernel(side_ref, left_ref, right_ref, lx1_ref, lx2_ref, ix1_ref, ix2_ref, out1_ref, out2_ref):
+    nx, H = left_ref.shape[0:2]
+    ny = lx1_ref.shape[1]
+    side = side_ref[0]
+    even = side_ref[1] == 0
+    ext = nx + 2 * H
+    low = slice(0, H)
+    high = slice(ny - H, ny)
+    for turn, out in ((True, out1_ref), (False, out2_ref)):
+        up = even if turn else jnp.logical_not(even)
+        out[H : nx + H] = jnp.where(up, right_ref[...], left_ref[...])
+        for at, step, one, two in (
+            (0, nx + H, lx1_ref, lx2_ref),
+            (ext, H, ix1_ref.at[0], ix2_ref.at[0]),
+            (ext + 2 * H, H, ix1_ref.at[1], ix2_ref.at[1]),
+        ):
+            out[pl.ds(at + (1 - side) * step, H)] = jnp.where(up, one[:, high, :], one[:, low, :])
+            out[pl.ds(at + side * step, H)] = jnp.where(up, two[:, high, :], two[:, low, :])
+
+
+def edges(side, left, right, lx1, lx2, ix1, ix2):
+    vmem, _, _ = specs()
+    nx, H, nz = left.shape
+    out = jax.ShapeDtypeStruct((nx + 6 * H, H, nz), f32)
+    return pl.pallas_call(
+        edges_kernel,
+        out_shape=(out, out),
+        in_specs=[scalars()] + [vmem] * 6,
+        out_specs=(vmem, vmem),
+        compiler_params=pltpu.CompilerParams(vmem_limit_bytes=16 << 20),
+        name="edges",
+    )(side, left, right, lx1, lx2, ix1, ix2)
+
+
+def jacobi(side, level, flag, divergence, halo):
     vmem, hbm, _ = specs()
     nx, ny, nz = divergence.shape
     ext = (nx + 2 * HALO, 2, ny + 2 * ROWS, 128)
-    lxl, lxh, lyl, lyh = level_halo
-    ixl, ixh, iyl, iyh = input_halo
     return pl.pallas_call(
         jacobi_kernel,
         out_shape=jax.ShapeDtypeStruct((nx, ny, nz), f32),
-        in_specs=[hbm] * 7 + [vmem] * 4,
+        in_specs=[scalars()] + [hbm] * 7 + [vmem] * (len(halo) - 4),
         out_specs=vmem,
-        scratch_shapes=[pltpu.VMEM(ext, f32)] * 6 + [pltpu.SemaphoreType.DMA((3, 3, 2))],
+        scratch_shapes=[pltpu.VMEM(ext, f32)] * 6
+        + [pltpu.VMEM((nx, 2, ny, 128), jnp.int32), pltpu.SemaphoreType.DMA((9, 2))],
         compiler_params=pltpu.CompilerParams(vmem_limit_bytes=48 << 20),
         name="jacobi",
-    )(level, kind, divergence, lxl, lxh, ixl, ixh, lyl, lyh, iyl, iyh)
+    )(side, level, flag, divergence, *halo)
 
 
 def spread_matrix():
@@ -509,41 +638,33 @@
     return hit.astype(jnp.bfloat16)
 
 
-def shifts(axis):
+def swap(axis, first, second):
     count = lax.axis_size(axis)
-    forward = [(i, i + 1) for i in range(count - 1)]
-    return forward, [(j, i) for i, j in forward]
-
-
-def swap(axis, low_part, high_part):
-    forward, backward = shifts(axis)
-    return lax.ppermute(high_part, axis, forward), lax.ppermute(low_part, axis, backward)
-
-
-def halo_y(block, xl, xh):
-    H = HALO
-    low = jnp.concatenate([xl[..., :H, :], block[..., :H, :], xh[..., :H, :]], axis=-3)
-    high = jnp.concatenate([xl[..., -H:, :], block[..., -H:, :], xh[..., -H:, :]], axis=-3)
-    return swap("gy", low, high)
+    arrived = []
+    for part, start in ((first, 0), (second, 1)):
+        pairs = []
+        for i in range(start, count - 1, 2):
+            pairs += [(i, i + 1), (i + 1, i)]
+        arrived.append(lax.ppermute(part, axis, pairs))
+    return arrived
 
 
 def per_device(particle_pos, tile_dest, tile_block, fluid_flag, divergence):
     nx, ny, nz = divergence.shape
     bricks = lax.axis_size("gx") * lax.axis_size("gy")
-
-    kind = 5.0 - 4.0 * fluid_flag.astype(f32)
-    pair = (kind, divergence)
-    ixl, ixh = swap("gx", jnp.stack([v[:HALO] for v in pair]), jnp.stack([v[-HALO:] for v in pair]))
-    edge = jnp.stack([jnp.concatenate([v[:, :HALO], v[:, -HALO:]], axis=1) for v in pair])
-    iyl, iyh = halo_y(edge, ixl, ixh)
+    side = jnp.stack([lax.axis_index("gx") % 2, lax.axis_index("gy") % 2]).astype(jnp.int32)
 
     send = pack(tile_dest[:, 0], tile_block, particle_pos, bricks)
+    send, flag, div = lax.optimization_barrier((send, fluid_flag, divergence))
     arrived = lax.all_to_all(send, ("gx", "gy"), split_axis=0, concat_axis=0, tiled=True)
-    arrived, iyl, iyh = lax.optimization_barrier((arrived, iyl, iyh))
-    level, low, high = splat(arrived, nx, ny, nz)
-    lxl, lxh = swap("gx", low, high)
-    lyl, lyh = halo_y(level, lxl, lxh)
-    pressure = jacobi(level, kind, divergence, (lxl, lxh, lyl, lyh), (ixl, ixh, iyl, iyh))
+    first, second, face1, face2 = strips(side, flag, div)
+    ix1, ix2 = swap("gx", first, second)
+    iy1, iy2 = swap("gy", face1, face2)
+    arrived, iy1, iy2 = lax.optimization_barrier((arrived, iy1, iy2))
+    level, sizes, first, second, left, right = splat(side, arrived, nx, ny, nz)
+    lx1, lx2 = swap("gx", first, second)
+    ly1, ly2 = swap("gy", *edges(side, left, right, lx1, lx2, ix1, ix2))
+    pressure = jacobi(side, sizes, flag, div, (lx1, lx2, ix1, ix2, ly1, ly2, iy1, iy2))
     return (level, pressure)
 
 

time: 150 us -> 117 us (0.78)
  the two profiles are of different devices: /device:TPU:3 before, /device:TPU:13 now
where the time goes in v4:
time: 117 us; the launch traced here: 116 us
  starting transfers between devices  54.2 us (46%)
  Pallas kernels  52.7 us (45%)
  waiting for transfers between devices  7.41 us (6%)
    ppermute x8, starting transfers between devices, swap(): arrived.append(lax.ppermute(part, axis, pairs))  43.5 us
    pallas_call x1, Pallas kernels, splat(): pl.pallas_call(splat_kernel, out_shape=(jax.ShapeDtypeStruct((nx, ny, nz)...  29.7 us
    pallas_call x1, Pallas kernels, jacobi(): pl.pallas_call(jacobi_kernel, out_shape=jax.ShapeDtypeStruct((nx, ny, nz)...  15 us
    all_to_all x1, starting transfers between devices, per_device(): lax.all_to_all(send, ('gx', 'gy'), split_axis=0, concat_axis=0, tiled=True)  10.7 us
    ppermute x8, waiting for transfers between devices, swap(): arrived.append(lax.ppermute(part, axis, pairs))  7.41 us
    pallas_call x1, Pallas kernels, pack(): pl.pallas_call(pack_kernel, out_shape=jax.ShapeDtypeStruct((bricks * 2, 4...  3.95 us
    pallas_call x1, Pallas kernels, strips(): pl.pallas_call(strips_kernel, out_shape=(strip, strip, edge, edge), in_sp...  3.49 us
  transfers between devices with their start and end apart: 9, of which 2 were waited for; matrix products, arithmetic and copies ran while one was open for 1% of the time, Pallas kernels for 29%

profile of v4, /device:TPU:13, one launch (start us, length us, event | category | flops | bytes accessed | tf_op | source)
XLA Modules:
  0.0 115.9 jit_solution(5379573898505613160)
XLA Ops:
  0.6 4.0 %pack.1 = f32[256,4,128]{2,1,0:T(4,128)} custom-call(s32[128]{0:T(128)} %bitcast.3, s32[128]{0:T(128)} %block_in.1, f32[3,16384]{1,0:T(4,128)} %pos_in.1), custom_call_target="tpu_custom_call" | custom-call | tf_op jit(solution)/shard_map/pack/pallas_call | solution.py:527
  4.6 10.7 %all-to-all-start = ((f32[256,4,128]{2,1,0:T(4,128)}), f32[256,4,128]{2,1,0:T(4,128)S(1)}, u32[]{:S(2)}, u32[]{:S(2)}) async-start(f32[256,4,128]{2,1,0:T(4,128)} %pack.1), calls=%async_computation | async-start | bytes 1048576 | tf_op jit(solution)/shard_map/all_to_all | solution.py:659
  15.3 0.6 pad_add_fusion.side_ref
  15.9 0.0 copy-start
  15.9 3.5 %strips.1 = (f32[2,4,64,256]{3,2,1,0:T(8,128)}, f32[2,4,64,256]{3,2,1,0:T(8,128)}, f32[2,32,4,256]{3,2,1,0:T(4,128)}, f32[2,32,4,256]{3,2,1,0:T(4,128)}) custom-call(s32[2]{0:T(128)} %pad_add_fusion.side_ref, s32[32,64,256]{2,1,0:T(8,128)} %flag_ref, f32[32,64,256]{2,1,0:T(8,128)} %div_ref), custom_call_target="tpu_custom_call" | custom-call | tf_op jit(solution)/shard_map/strips/pallas_call | solution.py:224
  19.4 0.4 collective-permute-start
  19.9 3.1 %collective-permute-start.1 = (f32[2,32,4,256]{3,2,1,0:T(4,128)}, f32[2,32,4,256]{3,2,1,0:T(4,128)S(1)}, u32[]{:S(2)}, u32[]{:S(2)}) collective-permute-start(f32[2,32,4,256]{3,2,1,0:T(4,128)} %get-tuple-element.24), channel_id=1, source_target_pairs={{1,2},{2,1},{3,4},{4,3},{5,6},{6,5},{9,10},{10,9},{11,12},{12,11},... | collective-permute-start | bytes 786440 | tf_op jit(solution)/shard_map/ppermute | solution.py:648
  23.0 1.5 %collective-permute-start.4 = (f32[2,4,64,256]{3,2,1,0:T(8,128)}, f32[2,4,64,256]{3,2,1,0:T(8,128)S(1)}, u32[]{:S(2)}, u32[]{:S(2)}) collective-permute-start(f32[2,4,64,256]{3,2,1,0:T(8,128)} %get-tuple-element.30), channel_id=1, source_target_pairs={{0,8},{8,0},{16,24},{24,16},{32,40},{40,32},{48,56},{56,48},{64,72... | collective-permute-start | bytes 1572872 | tf_op jit(solution)/shard_map/ppermute | solution.py:648
  24.5 3.9 %collective-permute-start.5 = (f32[2,4,64,256]{3,2,1,0:T(8,128)}, f32[2,4,64,256]{3,2,1,0:T(8,128)S(1)}, u32[]{:S(2)}, u32[]{:S(2)}) collective-permute-start(f32[2,4,64,256]{3,2,1,0:T(8,128)} %get-tuple-element.31), channel_id=1, source_target_pairs={{8,16},{16,8},{24,32},{32,24},{40,48},{48,40},{56,64},{64,56},{72,... | collective-permute-start | bytes 1572872 | tf_op jit(solution)/shard_map/ppermute | solution.py:648
  28.5 0.1 and_convert_fusion.spread_ref
  28.7 0.0 collective-permute-done.iy1_ref
  28.7 0.0 collective-permute-done.1.iy2_ref
  28.7 0.0 all-to-all-done.rec_ref
  28.7 0.0 copy-done
  28.7 29.7 %splat.1 = (f32[32,64,256]{2,1,0:T(8,128)}, f32[32,2,64,128]{3,2,1,0:T(8,128)S(1)}, f32[4,64,256]{2,1,0:T(8,128)S(1)}, f32[4,64,256]{2,1,0:T(8,128)S(1)}, f32[32...) custom-call(s32[2]{0:T(128)S(1)} %copy-done, bf16[128,384]{1,0:T(8,128)(2,1)S(1)} %and_convert_fusion.spread_ref, ...), custom_call_target="tpu_custom_call" | custom-call | tf_op jit(solution)/shard_map/splat/pallas_call | solution.py:551
  58.4 1.0 collective-permute-start.2
  59.3 25.8 %collective-permute-start.3 = (f32[4,64,256]{2,1,0:T(8,128)S(1)}, f32[4,64,256]{2,1,0:T(8,128)S(1)}, u32[]{:S(2)}, u32[]{:S(2)}) collective-permute-start(f32[4,64,256]{2,1,0:T(8,128)S(1)} %get-tuple-element.29), channel_id=1, source_target_pairs={{8,16},{16,8},{24,32},{32,24},{40,48},{48,40},{56,64},{64,56},{72,... | collective-permute-start | bytes 786440 | tf_op jit(solution)/shard_map/ppermute | solution.py:648
  85.2 0.0 collective-permute-done.4.ix1_ref
  85.2 0.0 collective-permute-done.5.ix2_ref
  85.2 0.0 collective-permute-done.2.lx1_ref
  85.2 3.7 %collective-permute-done.3.lx2_ref = f32[4,64,256]{2,1,0:T(8,128)S(1)} collective-permute-done((f32[4,64,256]{2,1,0:T(8,128)S(1)}, f32[4,64,256]{2,1,0:T(8,128)S(1)}, u32[]{:S(2)}, u32[]{:S(2)}) %collective-permute-start.3) | collective-permute-done | bytes 262176 | tf_op jit(solution)/shard_map/ppermute | solution.py:648
  88.9 0.6 edges.1
  89.5 0.1 collective-permute-start.6
  89.6 7.5 %collective-permute-start.7 = (f32[56,4,256]{2,1,0:T(4,128)S(1)}, f32[56,4,256]{2,1,0:T(4,128)S(1)}, u32[]{:S(2)}, u32[]{:S(2)}) collective-permute-start(f32[56,4,256]{2,1,0:T(4,128)S(1)} %get-tuple-element.35), channel_id=1, source_target_pairs={{1,2},{2,1},{3,4},{4,3},{5,6},{6,5},{9,10},{10,9},{11,12},{12,11},... | collective-permute-start | bytes 688136 | tf_op jit(solution)/shard_map/ppermute | solution.py:648
  97.2 0.0 collective-permute-done.6.ly1_ref
  97.2 3.7 %collective-permute-done.7.ly2_ref = f32[56,4,256]{2,1,0:T(4,128)S(1)} collective-permute-done((f32[56,4,256]{2,1,0:T(4,128)S(1)}, f32[56,4,256]{2,1,0:T(4,128)S(1)}, u32[]{:S(2)}, u32[]{:S(2)}) %collective-permute-start.7) | collective-permute-done | bytes 229408 | tf_op jit(solution)/shard_map/ppermute | solution.py:648
  100.9 15.0 %jacobi.1 = f32[32,64,256]{2,1,0:T(8,128)} custom-call(s32[2]{0:T(128)S(1)} %copy-done, f32[32,2,64,128]{3,2,1,0:T(8,128)S(1)} %get-tuple-element.27.level_ref, s32[32,64,256]{2,1,0:T(8,128)} %flag_ref, f32[32,64,256]{2,1,0:T(8,128)} %div_ref, f32[4,64,256]{2,1,0:T(8,128)S(1)} %collective-permute-done.2.lx1_ref, ...), custom_call_target="tpu_custom_call" | custom-call | tf_op jit(solution)/shard_map/jacobi/pallas_call | solution.py:620
  (3 shorter events, 0.0 us)
Async XLA Ops:
  4.6 24.1 %all-to-all-start = ((f32[256,4,128]{2,1,0:T(4,128)}), f32[256,4,128]{2,1,0:T(4,128)S(1)}, u32[]{:S(2)}, u32[]{:S(2)}) async-start(f32[256,4,128]{2,1,0:T(4,128)} %pack.1), calls=%async_computation | async-start | bytes 1048576 | tf_op jit(solution)/shard_map/all_to_all | solution.py:659
  15.9 12.8 %copy-start = (s32[2]{0:T(128)S(1)}, s32[2]{0:T(128)}, u32[]{:S(2)}) copy-start(s32[2]{0:T(128)} %pad_add_fusion.side_ref) | copy-start | bytes 28
  19.4 9.2 %collective-permute-start = (f32[2,32,4,256]{3,2,1,0:T(4,128)}, f32[2,32,4,256]{3,2,1,0:T(4,128)S(1)}, u32[]{:S(2)}, u32[]{:S(2)}) collective-permute-start(f32[2,32,4,256]{3,2,1,0:T(4,128)} %get-tuple-element.23), channel_id=1, source_target_pairs={{0,1},{1,0},{2,3},{3,2},{4,5},{5,4},{6,7},{7,6},{8,9},{9,8},{10,11... | collective-permute-start | bytes 786440 | tf_op jit(solution)/shard_map/ppermute | solution.py:648
  19.9 8.8 %collective-permute-start.1 = (f32[2,32,4,256]{3,2,1,0:T(4,128)}, f32[2,32,4,256]{3,2,1,0:T(4,128)S(1)}, u32[]{:S(2)}, u32[]{:S(2)}) collective-permute-start(f32[2,32,4,256]{3,2,1,0:T(4,128)} %get-tuple-element.24), channel_id=1, source_target_pairs={{1,2},{2,1},{3,4},{4,3},{5,6},{6,5},{9,10},{10,9},{11,12},{12,11},... | collective-permute-start | bytes 786440 | tf_op jit(solution)/shard_map/ppermute | solution.py:648
  23.0 62.2 %collective-permute-start.4 = (f32[2,4,64,256]{3,2,1,0:T(8,128)}, f32[2,4,64,256]{3,2,1,0:T(8,128)S(1)}, u32[]{:S(2)}, u32[]{:S(2)}) collective-permute-start(f32[2,4,64,256]{3,2,1,0:T(8,128)} %get-tuple-element.30), channel_id=1, source_target_pairs={{0,8},{8,0},{16,24},{24,16},{32,40},{40,32},{48,56},{56,48},{64,72... | collective-permute-start | bytes 1572872 | tf_op jit(solution)/shard_map/ppermute | solution.py:648
  24.5 60.6 %collective-permute-start.5 = (f32[2,4,64,256]{3,2,1,0:T(8,128)}, f32[2,4,64,256]{3,2,1,0:T(8,128)S(1)}, u32[]{:S(2)}, u32[]{:S(2)}) collective-permute-start(f32[2,4,64,256]{3,2,1,0:T(8,128)} %get-tuple-element.31), channel_id=1, source_target_pairs={{8,16},{16,8},{24,32},{32,24},{40,48},{48,40},{56,64},{64,56},{72,... | collective-permute-start | bytes 1572872 | tf_op jit(solution)/shard_map/ppermute | solution.py:648
  58.4 26.8 %collective-permute-start.2 = (f32[4,64,256]{2,1,0:T(8,128)S(1)}, f32[4,64,256]{2,1,0:T(8,128)S(1)}, u32[]{:S(2)}, u32[]{:S(2)}) collective-permute-start(f32[4,64,256]{2,1,0:T(8,128)S(1)} %get-tuple-element.28), channel_id=1, source_target_pairs={{0,8},{8,0},{16,24},{24,16},{32,40},{40,32},{48,56},{56,48},{64,72... | collective-permute-start | bytes 786440 | tf_op jit(solution)/shard_map/ppermute | solution.py:648
  59.3 29.6 %collective-permute-start.3 = (f32[4,64,256]{2,1,0:T(8,128)S(1)}, f32[4,64,256]{2,1,0:T(8,128)S(1)}, u32[]{:S(2)}, u32[]{:S(2)}) collective-permute-start(f32[4,64,256]{2,1,0:T(8,128)S(1)} %get-tuple-element.29), channel_id=1, source_target_pairs={{8,16},{16,8},{24,32},{32,24},{40,48},{48,40},{56,64},{64,56},{72,... | collective-permute-start | bytes 786440 | tf_op jit(solution)/shard_map/ppermute | solution.py:648
  89.5 7.6 %collective-permute-start.6 = (f32[56,4,256]{2,1,0:T(4,128)S(1)}, f32[56,4,256]{2,1,0:T(4,128)S(1)}, u32[]{:S(2)}, u32[]{:S(2)}) collective-permute-start(f32[56,4,256]{2,1,0:T(4,128)S(1)} %get-tuple-element.34), channel_id=1, source_target_pairs={{0,1},{1,0},{2,3},{3,2},{4,5},{5,4},{6,7},{7,6},{8,9},{9,8},{10,11... | collective-permute-start | bytes 688136 | tf_op jit(solution)/shard_map/ppermute | solution.py:648
  89.6 11.2 %collective-permute-start.7 = (f32[56,4,256]{2,1,0:T(4,128)S(1)}, f32[56,4,256]{2,1,0:T(4,128)S(1)}, u32[]{:S(2)}, u32[]{:S(2)}) collective-permute-start(f32[56,4,256]{2,1,0:T(4,128)S(1)} %get-tuple-element.35), channel_id=1, source_target_pairs={{1,2},{2,1},{3,4},{4,3},{5,6},{6,5},{9,10},{10,9},{11,12},{12,11},... | collective-permute-start | bytes 688136 | tf_op jit(solution)/shard_map/ppermute | solution.py:648
